TPU v7x, 128 devices: a whole 4x4x4 slice. The times are simulated.
128 devices in a mesh: lon: 16 (over z, y_hi, core), lat: 8 (over y_lo, x).
Axes of the slice: x: 4, y: 4 (y_hi: 2, y_lo: 2; y = y_hi * 2 + y_lo), z: 4, core: 2. Of those that a mesh axis runs over, the one named last changes fastest.
Arguments:
- ocean_state: bfloat16 [4, 75, 64, 4096], P(None, None, 'lat', 'lon'), may hold values from -6 to 6
- sea_mask: int32 [75, 64, 4096], P(None, 'lat', 'lon'), may hold values from 0 to 1
- fold_partner: int32 [4096], P('lon'), may hold values from 0 to 4095, as said below
- first_kernel: bfloat16 [9, 256, 75], replicated, may hold values from -0.25 to 0.25
- first_bias: float32 [256], replicated, may hold values from -3 to 3
- second_kernel: bfloat16 [9, 256, 256], replicated, may hold values from -0.125 to 0.125
- second_bias: float32 [256], replicated, may hold values from -3 to 3
Outputs:
- tendency: bfloat16 [4, 256, 64, 4096], P(None, None, 'lat', 'lon')
Inputs may be any that keep to these rules, and one draw needn't show every extreme that they name: sea_mask is 0 or 1 and never rises with level at a cell; fold_partner[j] = (s - j) mod 4096 for one whole number s.
All inputs are finite; a program needn't handle non-finite values.
Results may differ from a plain program's by a relative error of at most 0.0039.
Values may be sent and summed in bfloat16 or wider, within the bound.
A program may use at most 192 MiB of HBM per device.

v0:
```python
import jax
import jax.numpy as jnp
from jax import lax
from jax.sharding import PartitionSpec as P


def with_halo(block, sides, width, periodic):
    for axis, dim in sides:
        count = lax.axis_size(axis)
        forward = [(i, i + 1) for i in range(count - 1)]
        if periodic:
            forward.append((count - 1, 0))
        backward = [(target, source) for source, target in forward]
        low = lax.ppermute(
            lax.slice_in_dim(block, block.shape[dim] - width, None, axis=dim), axis, forward
        )
        high = lax.ppermute(lax.slice_in_dim(block, 0, width, axis=dim), axis, backward)
        block = jnp.concatenate([low, block, high], axis=dim)
    return block


def fold_by_gather(top_rows, fold_partner):
    shard_piece = lax.all_gather(top_rows, "lon", axis=3, tiled=True)
    col_ids = jnp.arange(shard_piece.shape[3], dtype=jnp.int32)
    selector = (fold_partner[:, None] == col_ids[None, :]).astype(jnp.bfloat16)
    gathered = jnp.einsum(
        "bcrk,wk->bcrw", shard_piece, selector, preferred_element_type=jnp.float32
    )
    return gathered.astype(jnp.bfloat16)


def fold_rows_over(top_rows, fold_partner):
    return fold_by_gather(top_rows, fold_partner)


def extend_field(field, fold_partner):
    row_padded = with_halo(field, (("lat", 2),), 1, False)
    ghost_rows = fold_rows_over(field[:, :, -1:, :], fold_partner)
    is_top = lax.axis_index("lat") == lax.axis_size("lat") - 1
    row_padded = row_padded.at[:, :, -1:, :].set(
        jnp.where(is_top, ghost_rows, row_padded[:, :, -1:, :])
    )
    return with_halo(row_padded, (("lon", 3),), 1, True)


def convolve(padded, kernel):
    row_count = padded.shape[2] - 2
    col_count = padded.shape[3] - 2
    running = None
    for tap_row in range(3):
        for tap_col in range(3):
            window = padded[:, :, tap_row : tap_row + row_count, tap_col : tap_col + col_count]
            product = jnp.einsum(
                "oc,bcrw->borw",
                kernel[3 * tap_row + tap_col],
                window,
                preferred_element_type=jnp.float32,
            )
            running = product if running is None else running + product
    return running


def on_device(
    ocean_state, sea_mask, fold_partner, first_kernel, first_bias, second_kernel, second_bias
):
    masked = ocean_state * sea_mask.astype(jnp.bfloat16)[None]
    surface = sea_mask[0].astype(jnp.float32)
    first_out = (
        convolve(extend_field(masked, fold_partner), first_kernel) + first_bias[None, :, None, None]
    )
    hidden = (jax.nn.gelu(first_out) * surface).astype(jnp.bfloat16)
    second_out = (
        convolve(extend_field(hidden, fold_partner), second_kernel)
        + second_bias[None, :, None, None]
    )
    return (second_out * surface).astype(jnp.bfloat16)


def solution(mesh):
    return jax.shard_map(
        on_device,
        mesh=mesh,
        in_specs=(P(None, None, "lat", "lon"), P(None, "lat", "lon"), P("lon"), P(), P(), P(), P()),
        out_specs=P(None, None, "lat", "lon"),
        check_vma=False,
    )
```

profile of v0, /device:TPU:14, one launch (start us, length us, event | category | flops | bytes accessed | tf_op | source)
XLA Modules:
  0.0 299.1 jit_solution(12966084208773989806)
XLA Ops:
  16.2 4.3 %collective-permute-done = bf16[4,75,1,256]{3,1,0,2:T(8,128)(2,1)S(1)} collective-permute-done((bf16[4,75,1,256]{3,1,0,2:T(8,128)(2,1)}, bf16[4,75,1,256]{3,1,0,2:T(8,128)(2,1)S(1)}, u32[]{:S(2)}, u32[]{:S(2)}) %collective-permute-start) | collective-permute-done | bytes 153632 | tf_op jit(solution)/shard_map/ppermute | solution.py:14
  20.8 40.3 %all-gather.3.cloned.1.call-done = bf16[4,75,1,4096]{3,1,0,2:T(8,128)(2,1)} async-done(((bf16[4,75,1,256]{3,1,0,2:T(8,128)(2,1)}), bf16[4,75,1,4096]{3,1,0,2:T(8,128)(2,1)}) %all-gather.3.cloned.1.call-update) | async-done | bytes 2457616 | tf_op jit(solution)/shard_map/all_gather | solution.py:23
  65.4 5.1 %collective-permute-start.3 = (bf16[4,75,10,1]{1,0,3,2:T(4,128)(2,1)S(1)}, bf16[4,75,10,1]{1,0,3,2:T(4,128)(2,1)S(1)}, u32[]{:S(2)}, u32[]{:S(2)}) collective-permute-start(bf16[4,75,10,1]{1,0,3,2:T(4,128)(2,1)S(1)} %copy.27), channel_id=1, source_target_pairs={{8,0},{16,8},{24,16},{32,24},{40,32},{48,40},{56,48},{64,56},{72,6... | collective-permute-start | bytes 18008 | tf_op jit(solution)/shard_map/ppermute | solution.py:17
  72.9 5.1 %pad_maximum_fusion.8 = (bf16[4,75,8,256]{3,1,0,2:T(8,128)(2,1)}, bf16[4,75,8,256]{3,1,0,2:T(8,128)(2,1)S(1)}, bf16[4,75,8,256]{3,1,0,2:T(8,128)(2,1)}, bf16[4,7...) fusion(bf16[4,75,10,1]{3,1,0,2:T(8,128)(2,1)S(1)} %copy.28, ...), kind=kLoop, calls=%fused_computation.56 | loop fusion | flops 14745600 | bytes 18268160 | tf_op jit(solution)/shard_map/concatenate | solution.py:18
  81.5 4.5 %fusion.48 = f32[4,8,256,256]{3,2,1,0:T(8,128)} fusion(bf16[4,75,8,256]{3,1,0,2:T(8,128)(2,1)S(1)} %get-tuple-element.39, bf16[9,256,75]{1,2,0:T(8,128)(2,1)S(1)} %copy-done.2), kind=kOutput, calls=%fused_computation.67 | convolution fusion | flops 314572800 | bytes 9740288 | tf_op jit(solution)/shard_map/oc,bcrw->borw/dot_general | solution.py:53
  86.0 4.5 %fusion.42 = f32[4,8,256,256]{3,2,1,0:T(8,128)} fusion(bf16[4,75,8,256]{3,1,0,2:T(8,128)(2,1)S(1)} %get-tuple-element.40, bf16[9,256,75]{1,2,0:T(8,128)(2,1)S(1)} %copy-done.2), kind=kOutput, calls=%fused_computation.61 | convolution fusion | flops 314572800 | bytes 9740288 | tf_op jit(solution)/shard_map/oc,bcrw->borw/dot_general | solution.py:53
  90.5 4.6 %fusion.54 = f32[4,8,256,256]{3,2,1,0:T(8,128)} fusion(bf16[4,75,8,256]{3,1,0,2:T(8,128)(2,1)S(1)} %get-tuple-element.41, bf16[9,256,75]{1,2,0:T(8,128)(2,1)S(1)} %copy-done.2), kind=kOutput, calls=%fused_computation.73 | convolution fusion | flops 314572800 | bytes 9740288 | tf_op jit(solution)/shard_map/oc,bcrw->borw/dot_general | solution.py:53
  95.1 4.6 %fusion.40 = f32[4,8,256,256]{3,2,1,0:T(8,128)} fusion(bf16[4,75,8,256]{3,1,0,2:T(8,128)(2,1)S(1)} %get-tuple-element.42, bf16[9,256,75]{1,2,0:T(8,128)(2,1)S(1)} %copy-done.2), kind=kOutput, calls=%fused_computation.59 | convolution fusion | flops 314572800 | bytes 9740288 | tf_op jit(solution)/shard_map/oc,bcrw->borw/dot_general | solution.py:53
  99.7 4.6 %fusion.46 = f32[4,8,256,256]{3,2,1,0:T(8,128)} fusion(bf16[4,75,8,256]{3,1,0,2:T(8,128)(2,1)S(1)} %get-tuple-element.43, bf16[9,256,75]{1,2,0:T(8,128)(2,1)S(1)} %copy-done.2), kind=kOutput, calls=%fused_computation.65 | convolution fusion | flops 314572800 | bytes 9740288 | tf_op jit(solution)/shard_map/oc,bcrw->borw/dot_general | solution.py:53
  104.2 4.5 %fusion.52 = f32[4,8,256,256]{3,2,1,0:T(8,128)} fusion(bf16[4,75,8,256]{3,1,0,2:T(8,128)(2,1)S(1)} %get-tuple-element.44, bf16[9,256,75]{1,2,0:T(8,128)(2,1)S(1)} %copy-done.2), kind=kOutput, calls=%fused_computation.71 | convolution fusion | flops 314572800 | bytes 9740288 | tf_op jit(solution)/shard_map/oc,bcrw->borw/dot_general | solution.py:53
  108.7 20.1 %fusion.8 = bf16[4,256,8,256]{1,3,2,0:T(8,128)(2,1)} fusion(f32[4,8,256,256]{3,2,1,0:T(8,128)} %fusion.40, f32[4,8,256,256]{3,2,1,0:T(8,128)} %fusion.42, f32[4,8,256,256]{3,2,1,0:T(8,128)S(1)} %fusion.44, f32[4,8,256,256]{3,2,1,0:T(8,128)} %fusion.46, f32[4,8,256,256]{3,2,1,0:T(8,128)} %fusion.48, f32[4,8,256,256]{3,2,1,0:T(8,128)S(1)} %fusion.50, ...), kind=kOutput, calls=%fused_computation.9 | convolution fusion | flops 354418688 | bytes 72582144 | tf_op jit(solution)/shard_map/oc,bcrw->borw/dot_general | solution.py:53
  135.1 9.7 %collective-permute-done.5 = bf16[4,256,1,256]{1,3,2,0:T(8,128)(2,1)S(1)} collective-permute-done((bf16[4,256,1,256]{1,3,2,0:T(8,128)(2,1)S(1)}, bf16[4,256,1,256]{1,3,2,0:T(8,128)(2,1)S(1)}, u32[]{:S(2)}, u32[]{:S(2)}) %collective-permute-start.5) | collective-permute-done | bytes 524320 | tf_op jit(solution)/shard_map/ppermute | solution.py:17
  144.8 4.4 %collective-permute-done.4 = bf16[4,256,1,256]{1,3,2,0:T(8,128)(2,1)S(1)} collective-permute-done((bf16[4,256,1,256]{1,3,2,0:T(8,128)(2,1)}, bf16[4,256,1,256]{1,3,2,0:T(8,128)(2,1)S(1)}, u32[]{:S(2)}, u32[]{:S(2)}) %collective-permute-start.4) | collective-permute-done | bytes 524320 | tf_op jit(solution)/shard_map/ppermute | solution.py:14
  149.1 5.2 %pad_maximum_fusion = bf16[4,256,10,256]{1,3,2,0:T(8,128)(2,1)} fusion(bf16[4,256,1,256]{1,3,2,0:T(8,128)(2,1)S(1)} %collective-permute-done.5, bf16[4,256,8,256]{1,3,2,0:T(8,128)(2,1)} %fusion.8, bf16[4,256,1,256]{1,3,2,0:T(8,128)(2,1)S(1)} %collective-permute-done.4), kind=kLoop, calls=%fused_computation.17 | loop fusion | flops 5242880 | bytes 10485760 | tf_op jit(solution)/shard_map/concatenate | solution.py:18
  154.3 54.3 %all-gather.5.cloned.1.call-done = bf16[4,256,1,4096]{1,3,2,0:T(8,128)(2,1)} async-done(((bf16[4,256,1,256]{1,3,2,0:T(8,128)(2,1)}), bf16[4,256,1,4096]{1,3,2,0:T(8,128)(2,1)}) %all-gather.5.cloned.1.call-update) | async-done | bytes 8388624 | tf_op jit(solution)/shard_map/all_gather | solution.py:23
  208.6 6.6 %fusion.71 = bf16[4,256,10,256]{1,3,2,0:T(8,128)(2,1)} fusion(bf16[4,256,10,256]{1,3,2,0:T(8,128)(2,1)} %pad_maximum_fusion, bf16[4,256,1,256]{1,3,2,0:T(8,128)(2,1)S(1)} %collective-permute-done.5, s32[256]{0:T(256)S(1)} %copy-done.5, bf16[4,256,1,4096]{1,3,2,0:T(8,128)(2,1)} %all-gather.5.cloned.1.call-done, pred[]{:T(512)S(6)} %eq.8), kind=kOutput, calls=%fused_computation.79 | convolution fusion | flops 2149056512 | bytes 9438209 | tf_op jit(solution)/shard_map/bcrk,wk->bcrw/dot_general | solution.py:26
  216.4 7.0 %fusion.97 = f32[4,8,256,256]{3,2,1,0:T(8,128)} fusion(bf16[4,256,10,256]{1,3,2,0:T(8,128)(2,1)} %fusion.71, bf16[9,256,256]{2,1,0:T(8,128)(2,1)S(1)} %copy-done.1), kind=kOutput, calls=%fused_computation.85 | convolution fusion | flops 1073741824 | bytes 13762560 | tf_op jit(solution)/shard_map/oc,bcrw->borw/dot_general | solution.py:53
  223.4 4.5 %fusion.101 = f32[4,8,256,256]{3,2,1,0:T(8,128)} fusion(bf16[4,256,10,256]{1,3,2,0:T(8,128)(2,1)S(1)} %bitcast.190, bf16[9,256,256]{2,1,0:T(8,128)(2,1)S(1)} %copy-done.1), kind=kOutput, calls=%fused_computation.89 | convolution fusion | flops 1073741824 | bytes 13762560 | tf_op jit(solution)/shard_map/oc,bcrw->borw/dot_general | solution.py:53
  228.2 4.5 %fusion.105 = f32[4,8,256,256]{3,2,1,0:T(8,128)} fusion(bf16[4,256,10,256]{1,3,2,0:T(8,128)(2,1)S(1)} %bitcast.190, bf16[9,256,256]{2,1,0:T(8,128)(2,1)S(1)} %copy-done.1), kind=kOutput, calls=%fused_computation.93 | convolution fusion | flops 1073741824 | bytes 13762560 | tf_op jit(solution)/shard_map/oc,bcrw->borw/dot_general | solution.py:53
  232.7 5.1 %collective-permute-start.7 = (bf16[4,256,10,1]{1,3,2,0:T(2,128)(2,1)S(1)}, bf16[4,256,10,1]{1,3,2,0:T(2,128)(2,1)S(1)}, u32[]{:S(2)}, u32[]{:S(2)}) collective-permute-start(bf16[4,256,10,1]{1,3,2,0:T(2,128)(2,1)S(1)} %get-tuple-element.29), channel_id=1, source_target_pairs={{8,0},{16,8},{24,16},{32,24},{40,32},{48,40},{56,48},{64,56},{72,6... | collective-permute-start | bytes 61448 | tf_op jit(solution)/shard_map/ppermute | solution.py:17
  245.8 4.5 %fusion.25 = f32[4,8,256,256]{3,2,1,0:T(8,128)} fusion(bf16[4,256,10,256]{1,3,2,0:T(8,128)(2,1)S(1)} %bitcast.190, bf16[4,256,10,1]{1,3,2,0:T(2,128)(2,1)S(1)} %collective-permute-done.6, bf16[9,256,256]{2,1,0:T(8,128)(2,1)S(1)} %copy-done.1), kind=kOutput, calls=%fused_computation.34 | convolution fusion | flops 1082130432 | bytes 13803520 | tf_op jit(solution)/shard_map/oc,bcrw->borw/dot_general | solution.py:53
  254.4 4.1 %fusion.12 = f32[4,8,256,256]{3,2,1,0:T(8,128)} fusion(bf16[4,256,10,256]{1,3,2,0:T(8,128)(2,1)S(1)} %bitcast.190, bf16[4,256,10,1]{1,3,2,0:T(2,128)(2,1)S(1)} %collective-permute-done.7, bf16[9,256,256]{2,1,0:T(8,128)(2,1)S(1)} %copy-done.1), kind=kOutput, calls=%fused_computation.23 | convolution fusion | flops 1082130432 | bytes 13803520 | tf_op jit(solution)/shard_map/oc,bcrw->borw/dot_general | solution.py:53
  258.5 26.0 %fusion.27 = bf16[4,256,8,256]{1,3,2,0:T(8,128)(2,1)} fusion(f32[8,256]{1,0:T(8,128)S(1)} %convert_bitcast_fusion, f32[256]{0:T(256)S(1)} %copy-done.4, f32[4,8,256,256]{3,2,1,0:T(8,128)} %fusion.97, f32[4,8,256,256]{3,2,1,0:T(8,128)} %fusion.25, f32[4,8,256,256]{3,2,1,0:T(8,128)} %fusion.12, f32[4,8,256,256]{3,2,1,0:T(8,128)} %fusion.101, ...), kind=kOutput, calls=%fused_computation.37 | convolution fusion | flops 1105199104 | bytes 76727296 | tf_op jit(solution)/shard_map/oc,bcrw->borw/dot_general | solution.py:53
  284.5 7.8 %copy.37 = bf16[4,256,8,256]{3,2,1,0:T(8,128)(2,1)} copy(bf16[4,256,8,256]{1,3,2,0:T(8,128)(2,1)} %fusion.27) | data formatting | bytes 8388608 | tf_op jit(solution)/shard_map/convert_element_type | solution.py:76
  (51 shorter events, 39.9 us)
Async XLA Ops:
  6.5 54.5 %copy-start.5 = (s32[256]{0:T(256)S(1)}, s32[256]{0:T(256)}, u32[]{:S(2)}) copy-start(s32[256]{0:T(256)} %param.13) | copy-start | bytes 3076
  6.5 54.5 %all-gather.3.cloned.1.call-start = ((), (), s32[]{:S(2)}) async-start(), calls=%async_computation | async-start | bytes 2785280 | tf_op jit(solution)/shard_map/all_gather | solution.py:23
  10.0 198.6 %all-gather.5.cloned.1.call-start = ((), (), s32[]{:S(2)}) async-start(), calls=%async_computation.1 | async-start | bytes 8912896 | tf_op jit(solution)/shard_map/all_gather | solution.py:23
  10.0 6.2 %collective-permute-start.1 = (bf16[4,75,1,256]{3,1,0,2:T(8,128)(2,1)S(1)}, bf16[4,75,1,256]{3,1,0,2:T(8,128)(2,1)S(1)}, u32[]{:S(2)}, u32[]{:S(2)}) collective-permute-start(bf16[4,75,1,256]{3,1,0,2:T(8,128)(2,1)S(1)} %get-tuple-element.48), channel_id=1, source_target_pairs={{1,0},{2,1},{3,2},{4,3},{5,4},{6,5},{7,6},{9,8},{10,9},{11,10},{12... | collective-permute-start | bytes 460808 | tf_op jit(solution)/shard_map/ppermute | solution.py:17
  12.8 7.8 %collective-permute-start = (bf16[4,75,1,256]{3,1,0,2:T(8,128)(2,1)}, bf16[4,75,1,256]{3,1,0,2:T(8,128)(2,1)S(1)}, u32[]{:S(2)}, u32[]{:S(2)}) collective-permute-start(bf16[4,75,1,256]{3,1,0,2:T(8,128)(2,1)} %get-tuple-element.47), channel_id=1, source_target_pairs={{0,1},{1,2},{2,3},{3,4},{4,5},{5,6},{6,7},{8,9},{9,10},{10,11},{11... | collective-permute-start | bytes 460808 | tf_op jit(solution)/shard_map/ppermute | solution.py:14
  65.1 7.3 %collective-permute-start.2 = (bf16[4,75,10,1]{1,0,3,2:T(4,128)(2,1)S(1)}, bf16[4,75,10,1]{1,0,3,2:T(4,128)(2,1)S(1)}, u32[]{:S(2)}, u32[]{:S(2)}) collective-permute-start(bf16[4,75,10,1]{1,0,3,2:T(4,128)(2,1)S(1)} %copy.23), channel_id=1, source_target_pairs={{0,8},{8,16},{16,24},{24,32},{32,40},{40,48},{48,56},{56,64},{64,7... | collective-permute-start | bytes 18008 | tf_op jit(solution)/shard_map/ppermute | solution.py:14
  65.4 6.5 %collective-permute-start.3 = (bf16[4,75,10,1]{1,0,3,2:T(4,128)(2,1)S(1)}, bf16[4,75,10,1]{1,0,3,2:T(4,128)(2,1)S(1)}, u32[]{:S(2)}, u32[]{:S(2)}) collective-permute-start(bf16[4,75,10,1]{1,0,3,2:T(4,128)(2,1)S(1)} %copy.27), channel_id=1, source_target_pairs={{8,0},{16,8},{24,16},{32,24},{40,32},{48,40},{56,48},{64,56},{72,6... | collective-permute-start | bytes 18008 | tf_op jit(solution)/shard_map/ppermute | solution.py:17
  78.0 2.2 copy-start
  78.0 2.2 copy-start.2
  104.2 4.5 %copy-start.3 = (f32[256]{0:T(256)S(1)}, f32[256]{0:T(256)}, u32[]{:S(2)}) copy-start(f32[256]{0:T(256)} %param.15) | copy-start | bytes 3076
  131.0 13.8 %collective-permute-start.5 = (bf16[4,256,1,256]{1,3,2,0:T(8,128)(2,1)S(1)}, bf16[4,256,1,256]{1,3,2,0:T(8,128)(2,1)S(1)}, u32[]{:S(2)}, u32[]{:S(2)}) collective-permute-start(bf16[4,256,1,256]{1,3,2,0:T(8,128)(2,1)S(1)} %get-tuple-element.32), channel_id=1, source_target_pairs={{1,0},{2,1},{3,2},{4,3},{5,4},{6,5},{7,6},{9,8},{10,9},{11,10},{12... | collective-permute-start | bytes 1572872 | tf_op jit(solution)/shard_map/ppermute | solution.py:17
  133.8 15.3 %collective-permute-start.4 = (bf16[4,256,1,256]{1,3,2,0:T(8,128)(2,1)}, bf16[4,256,1,256]{1,3,2,0:T(8,128)(2,1)S(1)}, u32[]{:S(2)}, u32[]{:S(2)}) collective-permute-start(bf16[4,256,1,256]{1,3,2,0:T(8,128)(2,1)} %get-tuple-element.31), channel_id=1, source_target_pairs={{0,1},{1,2},{2,3},{3,4},{4,5},{5,6},{6,7},{8,9},{9,10},{10,11},{11... | collective-permute-start | bytes 1572872 | tf_op jit(solution)/shard_map/ppermute | solution.py:14
  154.3 62.1 %copy-start.1 = (bf16[9,256,256]{2,1,0:T(8,128)(2,1)S(1)}, bf16[9,256,256]{2,1,0:T(8,128)(2,1)}, u32[]{:S(2)}) copy-start(bf16[9,256,256]{2,1,0:T(8,128)(2,1)} %param.16) | copy-start | bytes 3538948
  215.2 8.2 %slice-start = ((s8[5242880]{0:T(1024)(128)(4,1)}), s8[4194304]{0:T(1024)(128)(4,1)S(1)}, s32[]{:S(2)}) async-start(s8[5242880]{0:T(1024)(128)(4,1)} %bitcast.189), calls=%async_computation.2 | async-start | bytes 8388608
  216.4 7.0 %slice-start.1 = ((s8[5242880]{0:T(1024)(128)(4,1)}), s8[1048576]{0:T(1024)(128)(4,1)S(1)}, s32[]{:S(2)}) async-start(s8[5242880]{0:T(1024)(128)(4,1)} %bitcast.189), calls=%async_computation.3 | async-start | bytes 2097152
  227.9 9.9 %collective-permute-start.6 = (bf16[4,256,10,1]{1,3,2,0:T(2,128)(2,1)S(1)}, bf16[4,256,10,1]{1,3,2,0:T(2,128)(2,1)S(1)}, u32[]{:S(2)}, u32[]{:S(2)}) collective-permute-start(bf16[4,256,10,1]{1,3,2,0:T(2,128)(2,1)S(1)} %get-tuple-element.30), channel_id=1, source_target_pairs={{0,8},{8,16},{16,24},{24,32},{32,40},{40,48},{48,56},{56,64},{64,7... | collective-permute-start | bytes 61448 | tf_op jit(solution)/shard_map/ppermute | solution.py:14
  232.7 17.7 %collective-permute-start.7 = (bf16[4,256,10,1]{1,3,2,0:T(2,128)(2,1)S(1)}, bf16[4,256,10,1]{1,3,2,0:T(2,128)(2,1)S(1)}, u32[]{:S(2)}, u32[]{:S(2)}) collective-permute-start(bf16[4,256,10,1]{1,3,2,0:T(2,128)(2,1)S(1)} %get-tuple-element.29), channel_id=1, source_target_pairs={{8,0},{16,8},{24,16},{32,24},{40,32},{48,40},{56,48},{64,56},{72,6... | collective-permute-start | bytes 61448 | tf_op jit(solution)/shard_map/ppermute | solution.py:17
  254.4 4.1 %copy-start.4 = (f32[256]{0:T(256)S(1)}, f32[256]{0:T(256)}, u32[]{:S(2)}) copy-start(f32[256]{0:T(256)} %param.17) | copy-start | bytes 3076
Sparse Core Ops, SparseCore 0:
  10.1 50.8 all-gather.2
  131.1 77.4 all-gather.4
where the time goes:
time: 301 us; the launch traced here: 299 us
  matrix products  123 us (41%)
  waiting for transfers between devices  116 us (39%)
  starting transfers between devices  18.9 us (6%)
  local copies, waits for them, and re-layouts  14.1 us (5%)
  other arithmetic  13.9 us (5%)
  between operations  13.5 us (4%)
    dot_general x18, matrix products, convolve(): jnp.einsum('oc,bcrw->borw', kernel[3 * tap_row + tap_col], window, prefer...  113 us
    all_gather x2, waiting for transfers between devices, fold_by_gather(): shard_piece = lax.all_gather(top_rows, 'lon', axis=3, tiled=True)  94.5 us
    ppermute x4, starting transfers between devices, with_halo(): lax.ppermute(lax.slice_in_dim(block, 0, width, axis=dim), axis, backward)  15.7 us
    ppermute x4, waiting for transfers between devices, with_halo(): lax.ppermute(lax.slice_in_dim(block, 0, width, axis=dim), axis, backward)  12.5 us
    concatenate x3, other arithmetic, with_halo(): block = jnp.concatenate([low, block, high], axis=dim)  10.5 us
    dot_general x2, matrix products, fold_by_gather(): jnp.einsum('bcrk,wk->bcrw', shard_piece, selector, preferred_element_type...  9.43 us
    ppermute x4, waiting for transfers between devices, with_halo(): lax.ppermute(lax.slice_in_dim(block, block.shape[dim] - width, None, axis...  8.69 us
    convert_element_type x1, local copies, waits for them, and re-layouts, on_device(): return (second_out * surface).astype(jnp.bfloat16)  7.83 us
  transfers between devices with their start and end apart: 10, of which 7 were waited for; matrix products, arithmetic and copies ran while one was open for 8% of the time, Pallas kernels for 0%

commit v1 on v0

v1 whole, which is shorter than its diff:
```python
import functools

import jax
import jax.numpy as jnp
from jax import lax
from jax.experimental import pallas as pl
from jax.experimental.pallas import tpu as pltpu
from jax.sharding import PartitionSpec as P

F32 = jnp.float32
BF16 = jnp.bfloat16
MESH = pl.DeviceIdType.MESH
VMEM = pl.BlockSpec(memory_space=pltpu.VMEM)
SMEM = pl.BlockSpec(memory_space=pltpu.SMEM)

SAMPLES, CIN, ROWS, COLS, HID = 4, 75, 8, 256, 256
CPAD = 80
WIDE = SAMPLES * COLS
XROWS = ROWS + 4
HROWS = ROWS + 2
NLON, NLAT = 16, 8
LIMIT = 60 * 1024 * 1024


def lanes_of(shape):
    return lax.broadcasted_iota(jnp.int32, shape, len(shape) - 1)


def edge_pairs(x_ref, rows, left, right):
    pair = lax.shift_right_logical(lanes_of((CPAD, 128)), 1)
    for r in rows:
        for s in range(SAMPLES):
            row = x_ref[r, :, s * COLS : (s + 1) * COLS].astype(F32)
            at = 8 * r + 2 * s
            here = pair == at // 2
            left = jnp.where(here, pltpu.roll(row[:, :128], at, 1), left)
            right = jnp.where(here, pltpu.roll(row[:, 128:], (at + 2) % 128, 1), right)
    return left, right


def prepare(state_ref, mask_ref, x_ref, t_ref):
    for s in range(SAMPLES):
        for h in range(2):
            cut = slice(h * 128, (h + 1) * 128)
            t_ref[s, h, CIN * ROWS : (CIN + 1) * ROWS, :] = mask_ref[0, :, cut].astype(F32)
            t_ref[s, h, (CIN + 1) * ROWS :, :] = jnp.zeros(((CPAD - CIN - 1) * ROWS, 128), F32)
            masked = state_ref[s, :, :, cut].astype(F32) * mask_ref[:, :, cut].astype(F32)
            t_ref[s, h, : CIN * ROWS, :] = masked.reshape(CIN * ROWS, 128)
            for r in range(ROWS):
                at = s * COLS + h * 128
                x_ref[r + 2, :, at : at + 128] = t_ref[s, h, pl.ds(r, CPAD, stride=ROWS), :].astype(BF16)


def piece(i):
    return i // 8, (i // 2) % 4, i % 2


HALF = ((0, 48), (48, 32))


def exchange_kernel(
    state_ref, mask_ref, fold_ref, x_out, e_out,
    x_ref, t_ref, sp_ref, lp_ref, rp_ref, a_ref, y0_ref, y1_ref, s_ref, sp2_ref, p2_ref,
    row_send, row_recv, edge_send, edge_recv, f1_send, f1_recv, f2_send, f2_recv, f3_send, f3_recv,
):
    lon = lax.axis_index("lon")
    lat = lax.axis_index("lat")
    right, left = lax.rem(lon + 1, NLON), lax.rem(lon + NLON - 1, NLON)
    top = lat == NLAT - 1
    has = {-1: lat > 0, 0: None, 1: lat < NLAT - 1}

    def when(flag, fn):
        if flag is None:
            fn()
        else:
            pl.when(flag)(fn)

    barrier = pltpu.get_barrier_semaphore()

    def greet(at_lat, at_lon):
        pl.semaphore_signal(barrier, inc=1, device_id={"lat": at_lat, "lon": at_lon}, device_id_type=MESH)

    for d in (-1, 0, 1):
        def hello(d=d):
            if d:
                greet(lat + d, lon)
            greet(lat + d, left)
            greet(lat + d, right)
        when(has[d], hello)

    @pl.when(top)
    def _():
        for k in range(2, NLON - 1):
            greet(lat, lax.rem(lon + k, NLON))

    prepare(state_ref, mask_ref, x_ref, t_ref)
    zero = jnp.zeros((CPAD, 128), F32)
    own_left, own_right = edge_pairs(x_ref, range(2, 2 + ROWS), zero, zero)
    sp_ref[0] = own_left.astype(BF16)
    sp_ref[1] = own_right.astype(BF16)

    @pl.when(lat == 0)
    def _():
        x_ref[0:2] = jnp.zeros((2, CPAD, WIDE), BF16)
        lp_ref[0] = jnp.zeros((CPAD, 128), BF16)
        rp_ref[0] = jnp.zeros((CPAD, 128), BF16)

    @pl.when(jnp.logical_and(lat > 0, lat < NLAT - 1))
    def _():
        pl.semaphore_wait(barrier, 8)

    @pl.when(lat == 0)
    def _():
        pl.semaphore_wait(barrier, 5)

    @pl.when(top)
    def _():
        pl.semaphore_wait(barrier, 18)

    def to(src, dst, send, recv, at_lat, at_lon):
        return pltpu.make_async_remote_copy(
            src_ref=src, dst_ref=dst, send_sem=send, recv_sem=recv,
            device_id={"lat": at_lat, "lon": at_lon}, device_id_type=MESH,
        )

    def first_copy(i):
        row, s, half = piece(i)
        at, n = HALF[half]
        return to(
            x_ref.at[9 - row, pl.ds(at, n), pl.ds(s * COLS, COLS)], a_ref.at[lon, pl.ds(0, n)],
            f1_send.at[i], f1_recv.at[lon], lat, i,
        )

    my_row, my_s, my_half = piece(lon)

    def second_copy(d, half):
        at, n = HALF[half]
        return to(
            s_ref.at[d, pl.ds(0, n)],
            x_ref.at[10 + my_row, pl.ds(at, n), pl.ds(pl.multiple_of(my_s * COLS, COLS), COLS)],
            f2_send.at[d], f2_recv.at[lon], lat, d,
        )

    up = to(x_ref.at[pl.ds(8, 2)], x_ref.at[pl.ds(0, 2)], row_send.at[0], row_recv.at[0], lat + 1, lon)
    down = to(x_ref.at[pl.ds(2, 2)], x_ref.at[pl.ds(10, 2)], row_send.at[1], row_recv.at[1], lat - 1, lon)
    edge = {}
    for d in (-1, 0, 1):
        edge[d] = (
            to(sp_ref.at[0], rp_ref.at[1 - d], edge_send.at[d + 1], edge_recv.at[1 - d], lat + d, left),
            to(sp_ref.at[1], lp_ref.at[1 - d], edge_send.at[d + 4], edge_recv.at[4 - d], lat + d, right),
        )

    @pl.when(top)
    def _():
        for i in range(NLON):
            pl.when(i != lon)(lambda i=i: first_copy(i).start())

    for d in (-1, 0, 1):
        def go(d=d):
            edge[d][0].start()
            edge[d][1].start()
        when(has[d], go)
    pl.when(has[1])(lambda: up.start())
    pl.when(has[-1])(lambda: down.start())

    @pl.when(top)
    def _():
        for half in (0, 1):
            at, n = HALF[half]

            @pl.when(my_half == half)
            def _():
                mine = x_ref.at[9 - my_row, pl.ds(at, n), pl.ds(pl.multiple_of(my_s * COLS, COLS), COLS)]
                a_ref[lon, 0:n] = mine[...]
                if n < 48:
                    a_ref[:, n:] = jnp.zeros((NLON, 48 - n, COLS), BF16)
                for e in range(NLON):
                    def arrive(e=e):
                        to(a_ref.at[e, pl.ds(0, n)], a_ref.at[e, pl.ds(0, n)], f1_send.at[e], f1_recv.at[e], lat, e).wait_recv()
                    pl.when(e != lon)(arrive)

        start = fold_ref[0]
        turn = jnp.bitwise_and(start, COLS - 1)
        block = lax.shift_right_logical(start, 8)
        both = lax.broadcasted_iota(jnp.int32, (COLS, COLS), 0) + lax.broadcasted_iota(jnp.int32, (COLS, COLS), 1)
        pieces = a_ref[...].reshape(NLON * 48, COLS)
        for y_ref, target in ((y0_ref, turn), (y1_ref, turn + COLS)):
            choose = jnp.where(both == target, 1.0, 0.0).astype(BF16)
            y_ref[...] = jnp.dot(pieces, choose, preferred_element_type=F32).astype(BF16).reshape(NLON, 48, COLS)
        for d in range(NLON):
            b = jnp.bitwise_and(block + lon - d, NLON - 1)
            s_ref[d] = y0_ref[b] + y1_ref[jnp.bitwise_and(b + NLON - 1, NLON - 1)]
        for half in (0, 1):
            at, n = HALF[half]

            @pl.when(my_half == half)
            def _():
                for d in range(NLON):
                    pl.when(d != lon)(lambda d=d: second_copy(d, half).start())
                x_ref[10 + my_row, at : at + n, pl.ds(pl.multiple_of(my_s * COLS, COLS), COLS)] = s_ref[lon, 0:n]

    for d in (-1, 0, 1):
        def got(d=d):
            edge[-d][0].wait_recv()
            edge[-d][1].wait_recv()
        when(has[d], got)
    pl.when(has[1])(lambda: down.wait_recv())
    pl.when(has[-1])(lambda: up.wait_recv())

    @pl.when(top)
    def _():
        for e in range(NLON):
            row, s, half = piece(e)
            at, n = HALF[half]
            def arrive(e=e, row=row, s=s, at=at, n=n):
                there = x_ref.at[10 + row, pl.ds(at, n), pl.ds(s * COLS, COLS)]
                to(there, there, f2_send.at[e], f2_recv.at[e], lat, e).wait_recv()
            pl.when(e != lon)(arrive)

    far_left, far_right = edge_pairs(x_ref, (0, 1, 10, 11), own_left, own_right)

    @pl.when(top)
    def _():
        sp2_ref[0] = far_left.astype(BF16)
        sp2_ref[1] = far_right.astype(BF16)
        third = [
            to(sp2_ref.at[0], p2_ref.at[0], f3_send.at[0], f3_recv.at[0], lat, left),
            to(sp2_ref.at[1], p2_ref.at[1], f3_send.at[1], f3_recv.at[1], lat, right),
        ]
        for copy in third:
            copy.start()
        for copy in third:
            copy.wait()
        rp_ref[2] = pltpu.roll(p2_ref[0].astype(F32), 64, 1).astype(BF16)
        lp_ref[2] = pltpu.roll(p2_ref[1].astype(F32), 64, 1).astype(BF16)

    lane = lanes_of((CPAD, 128))

    def joined(ref):
        below = pltpu.roll(ref[0].astype(F32), 64, 1)
        above = pltpu.roll(ref[2].astype(F32), 64, 1)
        return jnp.where(lane < 16, below, jnp.where(lane < 80, ref[1].astype(F32), above))

    before, after = joined(lp_ref), joined(rp_ref)
    even = jnp.bitwise_and(lane, 1) == 0
    e_out[0] = jnp.where(even, before, far_right).astype(BF16)
    e_out[1] = jnp.where(even, pltpu.roll(before, 127, 1), pltpu.roll(after, 1, 1)).astype(BF16)
    e_out[2] = jnp.where(even, far_left, after).astype(BF16)
    x_out[...] = x_ref[...]

    pl.when(has[1])(lambda: up.wait_send())
    pl.when(has[-1])(lambda: down.wait_send())
    for d in (-1, 0, 1):
        def sent(d=d):
            edge[d][0].wait_send()
            edge[d][1].wait_send()
        when(has[d], sent)

    @pl.when(top)
    def _():
        for i in range(NLON):
            pl.when(i != lon)(lambda i=i: first_copy(i).wait_send())
        for half in (0, 1):
            @pl.when(my_half == half)
            def _():
                for d in range(NLON):
                    pl.when(d != lon)(lambda d=d: second_copy(d, half).wait_send())


def exchange(state, mask, fold):
    dma = pltpu.SemaphoreType.DMA
    return pl.pallas_call(
        exchange_kernel,
        out_shape=(
            jax.ShapeDtypeStruct((XROWS, CPAD, WIDE), BF16),
            jax.ShapeDtypeStruct((3, CPAD, 128), BF16),
        ),
        in_specs=[VMEM, VMEM, SMEM],
        out_specs=(VMEM, VMEM),
        scratch_shapes=[
            pltpu.VMEM((XROWS, CPAD, WIDE), BF16),
            pltpu.VMEM((SAMPLES, 2, CPAD * ROWS, 128), F32),
            pltpu.VMEM((2, CPAD, 128), BF16),
            pltpu.VMEM((3, CPAD, 128), BF16),
            pltpu.VMEM((3, CPAD, 128), BF16),
            pltpu.VMEM((NLON, 48, COLS), BF16),
            pltpu.VMEM((NLON, 48, COLS), BF16),
            pltpu.VMEM((NLON, 48, COLS), BF16),
            pltpu.VMEM((NLON, 48, COLS), BF16),
            pltpu.VMEM((2, CPAD, 128), BF16),
            pltpu.VMEM((2, CPAD, 128), BF16),
            dma((2,)), dma((2,)), dma((6,)), dma((6,)),
            dma((NLON,)), dma((NLON,)), dma((NLON,)), dma((NLON,)), dma((2,)), dma((2,)),
        ],
        compiler_params=pltpu.CompilerParams(collective_id=0, has_side_effects=True, vmem_limit_bytes=LIMIT),
    )(state, mask, fold)


def shift_rows(x_ref, e_ref, xb_ref, rows):
    lane = jnp.bitwise_and(lanes_of((CPAD, WIDE)), COLS - 1)
    for r in rows:
        row = x_ref[r].astype(F32)
        xb_ref[r, CPAD : 2 * CPAD, :] = x_ref[r]
        lower, upper = pltpu.roll(row, 1, 1), pltpu.roll(row, WIDE - 1, 1)
        mid = e_ref[1].astype(F32)
        firsts, lasts = [], []
        for s in range(SAMPLES):
            at = 8 * r + 2 * s
            firsts += [pltpu.roll(mid, (128 - at) % 128, 1), mid]
            lasts += [mid, pltpu.roll(mid, (127 - at - 1) % 128, 1)]
        xb_ref[r, :CPAD, :] = jnp.where(lane == 0, jnp.concatenate(firsts, 1), lower).astype(BF16)
        xb_ref[r, 2 * CPAD :, :] = jnp.where(lane == COLS - 1, jnp.concatenate(lasts, 1), upper).astype(BF16)


def gelu(x):
    return 0.5 * x * (1.0 + jnp.tanh(0.7978845608028654 * (x + 0.044715 * (x * x * x))))


def edge_hidden(e_ref, k1_ref, bias, top):
    taps = []
    for a in range(3):
        for b in range(3):
            taps.append(pltpu.roll(e_ref[b].astype(F32), (128 - 8 * a) % 128, 1))
    xe = jnp.concatenate(taps, 0).astype(BF16)
    plain = jnp.dot(k1_ref[0], xe, preferred_element_type=F32)
    turned = jnp.dot(k1_ref[1], xe, preferred_element_type=F32)
    lane = lanes_of((HID, 128))
    ghost = lane >= jnp.where(top, 72, 128)
    out = jnp.where(ghost, turned, plain) + bias
    surface = taps[4][CIN : CIN + 1, :]
    return gelu(out) * surface


def hidden_rows(x_ref, xb_ref, hb_ref, he_ref, k1_ref, bias, top, r):
    which = jnp.where(top, 1, 0) if r == HROWS - 1 else 0
    kernel = k1_ref[which]
    lane = jnp.bitwise_and(lanes_of((HID, 2 * COLS)), COLS - 1)
    taps = xb_ref[r : r + 3].reshape(9 * CPAD, WIDE)
    for pair in range(2):
        cut = slice(pair * 2 * COLS, (pair + 1) * 2 * COLS)
        out = jnp.dot(kernel, taps[:, cut], preferred_element_type=F32)
        surface = x_ref[r + 1, CIN - 11 : CPAD, cut].astype(F32)[11:12]
        out = gelu(out + jnp.concatenate([bias] * 4, 1)) * surface
        hb_ref[r, HID : 2 * HID, cut] = out.astype(BF16)
        lower, upper = pltpu.roll(out, 1, 1), pltpu.roll(out, 2 * COLS - 1, 1)
        firsts, lasts = [], []
        edge = he_ref[...]
        for s in (2 * pair, 2 * pair + 1):
            at = 8 * r + 2 * s
            firsts += [pltpu.roll(edge, (128 - at) % 128, 1), edge]
            lasts += [edge, pltpu.roll(edge, (127 - at - 1) % 128, 1)]
        hb_ref[r, :HID, cut] = jnp.where(lane == 0, jnp.concatenate(firsts, 1), lower).astype(BF16)
        hb_ref[r, 2 * HID :, cut] = jnp.where(lane == COLS - 1, jnp.concatenate(lasts, 1), upper).astype(BF16)


def output_rows(x_ref, hb_ref, k2_ref, of_ref, bias, r):
    kernel = jnp.concatenate([k2_ref[t] for t in range(9)], 1)
    taps = hb_ref[r : r + 3].reshape(9 * HID, WIDE)
    for pair in range(2):
        cut = slice(pair * 2 * COLS, (pair + 1) * 2 * COLS)
        out = jnp.dot(kernel, taps[:, cut], preferred_element_type=F32)
        surface = x_ref[r + 2, CIN - 11 : CPAD, cut].astype(F32)[11:12]
        out = (out + jnp.concatenate([bias] * 4, 1)) * surface
        for s in range(2):
            for h in range(2):
                at = s * COLS + h * 128
                of_ref[2 * pair + s, h, pl.ds(r, HID, stride=ROWS), :] = out[:, at : at + 128]


def wide_bias(ref):
    return jnp.transpose(jnp.broadcast_to(ref[...], (128, HID)))


def compute_kernel(x_ref, e_ref, k1_ref, b1_ref, k2_ref, b2_ref, out_ref, xb_ref, hb_ref, he_ref, of_ref):
    top = lax.axis_index("lat") == NLAT - 1
    bias1, bias2 = wide_bias(b1_ref), wide_bias(b2_ref)
    he_ref[...] = edge_hidden(e_ref, k1_ref, bias1, top)
    shift_rows(x_ref, e_ref, xb_ref, range(XROWS))
    for r in range(HROWS):
        hidden_rows(x_ref, xb_ref, hb_ref, he_ref, k1_ref, bias1, top, r)
    for r in range(ROWS):
        output_rows(x_ref, hb_ref, k2_ref, of_ref, bias2, r)
    for s in range(SAMPLES):
        for h in range(2):
            out_ref[s, :, :, h * 128 : (h + 1) * 128] = of_ref[s, h].reshape(HID, ROWS, 128).astype(BF16)


def compute(x, e, k1, b1, k2, b2):
    return pl.pallas_call(
        compute_kernel,
        out_shape=jax.ShapeDtypeStruct((SAMPLES, HID, ROWS, COLS), BF16),
        in_specs=[VMEM] * 6,
        out_specs=VMEM,
        scratch_shapes=[
            pltpu.VMEM((XROWS, 3 * CPAD, WIDE), BF16),
            pltpu.VMEM((HROWS, 3 * HID, WIDE), BF16),
            pltpu.VMEM((HID, 128), F32),
            pltpu.VMEM((SAMPLES, 2, HID * ROWS, 128), F32),
        ],
        compiler_params=pltpu.CompilerParams(vmem_limit_bytes=LIMIT),
    )(x, e, k1, b1, k2, b2)


def on_device(state, mask, fold, first_kernel, first_bias, second_kernel, second_bias):
    taps = jnp.pad(first_kernel, ((0, 0), (0, 0), (0, CPAD - CIN)))
    both = jnp.stack([taps, taps[::-1]])
    k1 = jnp.transpose(both, (0, 2, 1, 3)).reshape(2, HID, 9 * CPAD)
    x, e = exchange(state, mask, fold)
    return compute(x, e, k1, first_bias[None], second_kernel, second_bias[None])


def solution(mesh):
    return jax.shard_map(
        on_device,
        mesh=mesh,
        in_specs=(P(None, None, "lat", "lon"), P(None, "lat", "lon"), P("lon"), P(), P(), P(), P()),
        out_specs=P(None, None, "lat", "lon"),
        check_vma=False,
    )
```

time: 301 us -> 62 us (0.21)
  matrix products: 123 us -> 0 us
  waiting for transfers between devices: 116 us -> 0 us
  Pallas kernels: 0 us -> 59.5 us
  starting transfers between devices: 18.9 us -> 0 us
  other arithmetic: 13.9 us -> 0.07 us
  between operations: 13.5 us -> 0.03 us
  local copies, waits for them, and re-layouts: 14.1 us -> 2.22 us
    dot_general x20 -> x0, matrix products: 123 us -> none  [the longest x18 113 us: convolve(): jnp.einsum('oc,bcrw->borw', kernel[3 * tap_row + tap_col], window, prefer...]
    all_gather x2 -> x0, waiting for transfers between devices: 94.5 us -> none  [fold_by_gather(): shard_piece = lax.all_gather(top_rows, 'lon', axis=3, tiled=True)]
    pallas_call x0 -> x2, Pallas kernels: none -> 59.5 us  [the longest x1 35.1 us: exchange(): pl.pallas_call(exchange_kernel, out_shape=(jax.ShapeDtypeStruct((XROWS, C...]
    ppermute x8 -> x0, waiting for transfers between devices: 21.2 us -> none  [the longest x4 12.5 us: with_halo(): lax.ppermute(lax.slice_in_dim(block, 0, width, axis=dim), axis, backward)]
    ppermute x8 -> x0, starting transfers between devices: 18.9 us -> none  [the longest x4 15.7 us: with_halo(): lax.ppermute(lax.slice_in_dim(block, 0, width, axis=dim), axis, backward)]
    concatenate x3 -> x0, other arithmetic: 10.5 us -> none  [with_halo(): block = jnp.concatenate([low, block, high], axis=dim)]
    convert_element_type x2 -> x0, local copies, waits for them, and re-layouts: 7.89 us -> none  [the longest x1 7.83 us: on_device(): return (second_out * surface).astype(jnp.bfloat16)]
    slice x6 -> x0, local copies, waits for them, and re-layouts: 5.25 us -> none  [the longest x3 3.23 us: with_halo(): lax.slice_in_dim(block, block.shape[dim] - width, None, axis=dim)]
  transfers between devices with their start and end apart: 10 -> 0, of which waited for: 7 -> 0; matrix products, arithmetic and copies ran while one was open for 8% -> 0% of each run, Pallas kernels for 0% -> 0%
where the time goes in v1:
time: 62 us; the launch traced here: 61.8 us
  Pallas kernels  59.5 us (96%)
  local copies, waits for them, and re-layouts  2.22 us (4%)
    pallas_call x1, Pallas kernels, exchange(): pl.pallas_call(exchange_kernel, out_shape=(jax.ShapeDtypeStruct((XROWS, C...  35.1 us
    pallas_call x1, Pallas kernels, compute(): pl.pallas_call(compute_kernel, out_shape=jax.ShapeDtypeStruct((SAMPLES, H...  24.5 us

profile of v1, /device:TPU:14, one launch (start us, length us, event | category | flops | bytes accessed | tf_op | source)
XLA Modules:
  0.0 61.8 jit_solution(1003275302899384527)
XLA Ops:
  0.0 1.0 %pad_bitcast_fusion = (bf16[1,9,256,80]{2,3,1,0:T(8,128)(2,1)S(1)}, bf16[9,256,80]{1,2,0:T(8,128)(2,1)S(1)}) fusion(bf16[9,256,75]{1,2,0:T(8,128)(2,1)} %param.10), kind=kLoop, calls=%fused_computation.2 | loop fusion | bytes 1082880 | tf_op jit(solution)/shard_map/stack | solution.py:406
  1.1 0.1 pad_maximum_fusion
  1.2 1.2 %copy.9.k1_ref = bf16[2,256,720]{2,1,0:T(8,128)(2,1)} copy(bf16[2,256,720]{1,2,0:T(8,128)(2,1)S(1)} %bitcast.9) | data formatting | bytes 1474560 | tf_op jit(solution)/shard_map/reshape | solution.py:407
  2.3 35.1 %shard_map.73 = (bf16[12,80,1024]{2,1,0:T(8,128)(2,1)}, bf16[3,80,128]{2,1,0:T(8,128)(2,1)}) custom-call(bf16[4,75,8,256]{3,2,1,0:T(8,128)(2,1)} %state_ref.1, s32[75,8,256]{2,1,0:T(8,128)} %mask_ref.1, s32[256]{0:T(256)} %fold_ref.1), custom_call_target="tpu_custom_call" | custom-call | tf_op jit(solution)/shard_map/pallas_call | solution.py:272
  37.4 24.5 %shard_map.74 = bf16[4,256,8,256]{3,2,1,0:T(8,128)(2,1)} custom-call(bf16[12,80,1024]{2,1,0:T(8,128)(2,1)} %get-tuple-element.7.x_ref, bf16[3,80,128]{2,1,0:T(8,128)(2,1)} %get-tuple-element.8.e_ref, bf16[2,256,720]{2,1,0:T(8,128)(2,1)} %copy.9.k1_ref, f32[1,256]{1,0:T(1,128)} %bitcast.10, bf16[9,256,256]{2,1,0:T(8,128)(2,1)} %k2_ref.1, f32[1,256]{1,0:T(1,128)} %bitcast.11), custom_call_target="tpu_custom_call" | custom-call | tf_op jit(solution)/shard_map/pallas_call | solution.py:389
  (1 shorter events, 0.0 us)

commit v2 on v1

v2 whole, which is shorter than its diff:
```python
import functools

import jax
import jax.numpy as jnp
from jax import lax
from jax.experimental import pallas as pl
from jax.experimental.pallas import tpu as pltpu
from jax.sharding import PartitionSpec as P

F32 = jnp.float32
BF16 = jnp.bfloat16
MESH = pl.DeviceIdType.MESH
VMEM = pl.BlockSpec(memory_space=pltpu.VMEM)
SMEM = pl.BlockSpec(memory_space=pltpu.SMEM)

SAMPLES, CIN, ROWS, COLS, HID = 4, 75, 8, 256, 256
CPAD = 80
WIDE = SAMPLES * COLS
XROWS = ROWS + 4
HROWS = ROWS + 2
NLON, NLAT = 16, 8
LIMIT = 60 * 1024 * 1024


def lanes_of(shape):
    return lax.broadcasted_iota(jnp.int32, shape, len(shape) - 1)


def edge_pairs(x_ref, rows, pairs):
    pair = lax.shift_right_logical(lanes_of((CPAD, 128)), 1)
    pairs = list(pairs)
    for r in rows:
        for s in range(SAMPLES):
            row = x_ref[r, :, s * COLS : (s + 1) * COLS].astype(F32)
            at = 8 * r + 2 * s
            here = pair == at // 2
            for n, (half, by) in enumerate(((0, at), (0, at - 2), (1, at + 4), (1, at + 2))):
                part = pltpu.roll(row[:, half * 128 : half * 128 + 128], by % 128, 1)
                pairs[n] = jnp.where(here, part, pairs[n])
    return pairs


def prepare(state_ref, mask_ref, x_ref, t_ref):
    for s in range(SAMPLES):
        for h in range(2):
            cut = slice(h * 128, (h + 1) * 128)
            t_ref[s, h, CIN * ROWS : (CIN + 1) * ROWS, :] = mask_ref[0, :, cut].astype(F32)
            t_ref[s, h, (CIN + 1) * ROWS :, :] = jnp.zeros(((CPAD - CIN - 1) * ROWS, 128), F32)
            masked = state_ref[s, :, :, cut].astype(F32) * mask_ref[:, :, cut].astype(F32)
            t_ref[s, h, : CIN * ROWS, :] = masked.reshape(CIN * ROWS, 128)
            for r in range(ROWS):
                at = s * COLS + h * 128
                x_ref[r + 2, :, at : at + 128] = t_ref[s, h, pl.ds(r, CPAD, stride=ROWS), :].astype(BF16)


def piece(i):
    return i // 8, (i // 2) % 4, i % 2


HALF = ((0, 48), (48, 32))
EARLY = (2, 3, 4, 5)


def gelu(x):
    return 0.5 * x * (1.0 + jnp.tanh(0.7978845608028654 * (x + 0.044715 * (x * x * x))))


def wide_bias(ref):
    return jnp.transpose(jnp.broadcast_to(ref[...], (128, HID)))


def stack_taps(raw_ref, pad_ref, k1_ref, turned):
    lane = lanes_of((HID, 128))
    blocks = [None] * 6
    for t in range(9):
        if not turned:
            pad_ref[t, :, CIN:] = jnp.zeros((HID, 128 - CIN), F32)
            pad_ref[t, :, :CIN] = raw_ref[t].astype(F32)
        at = CPAD * (8 - t if turned else t)
        q, p = at // 128, at % 128
        moved = pltpu.roll(pad_ref[t], p, 1) if p else pad_ref[t]
        for block, keep in ((q, lane >= p), (q + 1, lane < p)):
            if block == q + 1 and p + CIN <= 128:
                continue
            part = jnp.where(keep, moved, 0.0)
            blocks[block] = part if blocks[block] is None else blocks[block] + part
    for n, block in enumerate(blocks):
        wide = min(128, 9 * CPAD - n * 128)
        k1_ref[1 if turned else 0, :, n * 128 : n * 128 + wide] = block[:, :wide].astype(BF16)


def shift_row(x_ref, xb_ref, r):
    row = x_ref[r].astype(F32)
    xb_ref[r, :CPAD, :] = pltpu.roll(row, 1, 1).astype(BF16)
    xb_ref[r, CPAD : 2 * CPAD, :] = x_ref[r]
    xb_ref[r, 2 * CPAD :, :] = pltpu.roll(row, WIDE - 1, 1).astype(BF16)


def hidden_row(x_ref, xb_ref, hb_ref, k1_ref, bias, which, r):
    kernel = k1_ref[which]
    taps = xb_ref[r : r + 3].reshape(9 * CPAD, WIDE)
    for pair in range(2):
        cut = slice(pair * 2 * COLS, (pair + 1) * 2 * COLS)
        out = jnp.dot(kernel, taps[:, cut], preferred_element_type=F32)
        surface = x_ref[r + 1, 64:CPAD, cut].astype(F32)[CIN - 64 : CIN - 63]
        out = gelu(out + jnp.concatenate([bias] * 4, 1)) * surface
        hb_ref[r, :HID, cut] = pltpu.roll(out, 1, 1).astype(BF16)
        hb_ref[r, HID : 2 * HID, cut] = out.astype(BF16)
        hb_ref[r, 2 * HID :, cut] = pltpu.roll(out, 2 * COLS - 1, 1).astype(BF16)


def output_row(x_ref, hb_ref, k2_ref, y_ref, bias, r):
    kernel = jnp.concatenate([k2_ref[t] for t in range(9)], 1)
    taps = hb_ref[r : r + 3].reshape(9 * HID, WIDE)
    for pair in range(2):
        cut = slice(pair * 2 * COLS, (pair + 1) * 2 * COLS)
        out = jnp.dot(kernel, taps[:, cut], preferred_element_type=F32)
        surface = x_ref[r + 2, 64:CPAD, cut].astype(F32)[CIN - 64 : CIN - 63]
        out = ((out + jnp.concatenate([bias] * 4, 1)) * surface).astype(BF16)
        y_ref[r, 2 * pair] = out[:, :COLS]
        y_ref[r, 2 * pair + 1] = out[:, COLS:]


def edge_columns(columns, k1_ref, k2_ref, bias1, bias2, top):
    lane = lanes_of((HID, 128))
    back = [[c if not a else pltpu.roll(c, 128 - 8 * a, 1) for a in range(3)] for c in columns]
    taps = jnp.concatenate(
        [jnp.concatenate([back[i + b][a] for a in range(3) for b in range(3)], 0).astype(BF16) for i in range(4)], 1
    )
    plain = jnp.dot(k1_ref[0], taps, preferred_element_type=F32)
    turned = jnp.dot(k1_ref[1], taps, preferred_element_type=F32)
    ghost = lane >= jnp.where(top, 72, 128)
    hidden = []
    for i in range(4):
        cut = slice(i * 128, (i + 1) * 128)
        out = jnp.where(ghost, turned[:, cut], plain[:, cut]) + bias1
        out = gelu(out) * back[i + 1][1][CIN : CIN + 1, :]
        hidden.append([out if not a else pltpu.roll(out, 128 - 8 * a, 1) for a in range(3)])
    taps = jnp.concatenate(
        [jnp.concatenate([hidden[i + b][a] for a in range(3) for b in range(3)], 0).astype(BF16) for i in range(2)], 1
    )
    kernel = jnp.concatenate([k2_ref[t] for t in range(9)], 1)
    out = jnp.dot(kernel, taps, preferred_element_type=F32)
    first, second = ((out[:, i * 128 : i * 128 + 128] + bias2) * back[i + 2][2][CIN : CIN + 1, :] for i in range(2))
    even = jnp.bitwise_and(lane, 1) == 0
    return jnp.where(even, first, pltpu.roll(second, 1, 1)), jnp.where(even, pltpu.roll(first, 127, 1), second)


def fold_kernel_parts(a_ref, y0_ref, y1_ref, s_ref, se_ref, fold_ref, lon):
    start = fold_ref[0]
    turn = jnp.bitwise_and(start, COLS - 1)
    block = lax.shift_right_logical(start, 8)
    source = lax.broadcasted_iota(jnp.int32, (COLS, COLS), 0)
    lane = lax.broadcasted_iota(jnp.int32, (COLS, COLS), 1)
    pieces = a_ref[...].reshape(NLON * 48, COLS)
    for y_ref, target in ((y0_ref, turn), (y1_ref, turn + COLS)):
        choose = jnp.where(source + lane == target, 1.0, 0.0).astype(BF16)
        y_ref[...] = jnp.dot(pieces, choose, preferred_element_type=F32).astype(BF16).reshape(NLON, 48, COLS)
    for d in range(NLON):
        b = jnp.bitwise_and(block + lon - d, NLON - 1)
        s_ref[d] = y0_ref[b] + y1_ref[jnp.bitwise_and(b + NLON - 1, NLON - 1)]
    group = lax.shift_right_logical(lane, 4)
    step = jnp.where(group >= 8, group - 16, group)
    k = jnp.bitwise_and(lane, 15)
    column = jnp.where(k < 2, k - 2, k + COLS - 2)
    hit = jnp.logical_and(k < 4, source == turn - column - COLS * step)
    outer = jnp.dot(pieces, jnp.where(hit, 1.0, 0.0).astype(BF16), preferred_element_type=F32).reshape(NLON, 48, COLS)
    total = jnp.zeros((48, COLS), F32)
    for e in range(NLON):
        total = total + pltpu.roll(outer[e], jnp.bitwise_and(16 * (block + lon - e), COLS - 1), 1)
    total = jnp.concatenate([total, jnp.zeros((80, COLS), F32)], 0)
    se_ref[...] = jnp.transpose(total).astype(BF16).reshape(NLON, 16, 128)


def fold_edges(fe_ref):
    sent = jnp.transpose(fe_ref[...].reshape(NLON * 16, 128).astype(F32)).astype(BF16)
    f = lax.broadcasted_iota(jnp.int32, (256, 512), 0)
    lane = lax.broadcasted_iota(jnp.int32, (256, 512), 1)
    to_lane, side, half = jnp.bitwise_and(lane, 127), jnp.bitwise_and(lane // 128, 1), lane // 256
    hit = jnp.logical_and(
        jnp.bitwise_and(f // 16, 1) == half,
        jnp.logical_and(
            jnp.bitwise_and(f, 15) == 2 * side + jnp.bitwise_and(to_lane, 1),
            to_lane // 2 == 40 + (f // 128) * 4 + jnp.bitwise_and(f // 32, 3),
        ),
    )
    got = jnp.dot(sent, jnp.where(hit, 1.0, 0.0).astype(BF16), preferred_element_type=F32)
    return [jnp.concatenate([got[:48, n : n + 128], got[:32, 256 + n : 384 + n]], 0) for n in (0, 128)]


def main_kernel(
    state_hbm, mask_hbm, fold_ref, k1_hbm, b1_ref, k2_hbm, b2_ref, y_hbm, edge_out,
    state_ref, mask_ref, k1_raw, k1_pad, k1_ref, k2_ref, x_ref, t_ref, xb_ref, hb_ref, y_ref,
    sp_ref, lp_ref, rp_ref, a_ref, y0_ref, y1_ref, s_ref, se_ref, fe_ref, ft_ref,
    load_sem, store_sem,
    row_send, row_recv, edge_send, edge_recv, f1_send, f1_recv, f2_send, f2_recv, f3_send, f3_recv,
):
    loads = [
        pltpu.make_async_copy(src, dst, load_sem.at[n])
        for n, (src, dst) in enumerate(((mask_hbm, mask_ref), (state_hbm, state_ref), (k1_hbm, k1_raw), (k2_hbm, k2_ref)))
    ]
    for load in loads:
        load.start()
    lon = lax.axis_index("lon")
    lat = lax.axis_index("lat")
    right, left = lax.rem(lon + 1, NLON), lax.rem(lon + NLON - 1, NLON)
    top = lat == NLAT - 1
    has = {-1: lat > 0, 0: None, 1: lat < NLAT - 1}

    def when(flag, fn):
        if flag is None:
            fn()
        else:
            pl.when(flag)(fn)

    barrier = pltpu.get_barrier_semaphore()

    def greet(at_lat, at_lon):
        pl.semaphore_signal(barrier, inc=1, device_id={"lat": at_lat, "lon": at_lon}, device_id_type=MESH)

    for d in (-1, 0, 1):
        def hello(d=d):
            if d:
                greet(lat + d, lon)
            greet(lat + d, left)
            greet(lat + d, right)
        when(has[d], hello)

    @pl.when(top)
    def _():
        for k in range(2, NLON - 1):
            greet(lat, lax.rem(lon + k, NLON))

    loads[0].wait()
    loads[1].wait()
    prepare(state_ref, mask_ref, x_ref, t_ref)
    pairs = edge_pairs(x_ref, range(2, 2 + ROWS), [jnp.zeros((CPAD, 128), F32)] * 4)
    sp_ref[0] = pairs[0].astype(BF16)
    sp_ref[1] = pairs[3].astype(BF16)
    loads[2].wait()
    stack_taps(k1_raw, k1_pad, k1_ref, False)
    bias1, bias2 = wide_bias(b1_ref), wide_bias(b2_ref)

    def hidden(r, which=0):
        hidden_row(x_ref, xb_ref, hb_ref, k1_ref, bias1, which, r)

    stores = []

    def output(r):
        output_row(x_ref, hb_ref, k2_ref, y_ref, bias2, r)
        stores.append(pltpu.make_async_copy(y_ref.at[r], y_hbm.at[:, r], store_sem.at[r]))
        stores[-1].start()

    for r in range(2, 2 + ROWS):
        shift_row(x_ref, xb_ref, r)
    for r in EARLY:
        hidden(r)

    @pl.when(lat == 0)
    def _():
        x_ref[0:2] = jnp.zeros((2, CPAD, WIDE), BF16)
        lp_ref[0] = jnp.zeros((CPAD, 128), BF16)
        rp_ref[0] = jnp.zeros((CPAD, 128), BF16)

    @pl.when(jnp.logical_and(lat > 0, lat < NLAT - 1))
    def _():
        pl.semaphore_wait(barrier, 8)

    @pl.when(lat == 0)
    def _():
        pl.semaphore_wait(barrier, 5)

    @pl.when(top)
    def _():
        pl.semaphore_wait(barrier, 18)

    def to(src, dst, send, recv, at_lat, at_lon):
        return pltpu.make_async_remote_copy(
            src_ref=src, dst_ref=dst, send_sem=send, recv_sem=recv,
            device_id={"lat": at_lat, "lon": at_lon}, device_id_type=MESH,
        )

    def first_copy(i):
        row, s, half = piece(i)
        at, n = HALF[half]
        return to(
            x_ref.at[9 - row, pl.ds(at, n), pl.ds(s * COLS, COLS)], a_ref.at[lon, pl.ds(0, n)],
            f1_send.at[i], f1_recv.at[lon], lat, i,
        )

    my_row, my_s, my_half = piece(lon)

    def second_copy(d, half):
        at, n = HALF[half]
        return to(
            s_ref.at[d, pl.ds(0, n)],
            x_ref.at[10 + my_row, pl.ds(at, n), pl.ds(pl.multiple_of(my_s * COLS, COLS), COLS)],
            f2_send.at[d], f2_recv.at[lon], lat, d,
        )

    def third_copy(d):
        return to(se_ref.at[d], fe_ref.at[lon], f3_send.at[d], f3_recv.at[lon], lat, d)

    up = to(x_ref.at[pl.ds(8, 2)], x_ref.at[pl.ds(0, 2)], row_send.at[0], row_recv.at[0], lat + 1, lon)
    down = to(x_ref.at[pl.ds(2, 2)], x_ref.at[pl.ds(10, 2)], row_send.at[1], row_recv.at[1], lat - 1, lon)
    edge = {}
    for d in (-1, 0, 1):
        edge[d] = (
            to(sp_ref.at[0], rp_ref.at[1 - d], edge_send.at[d + 1], edge_recv.at[1 - d], lat + d, left),
            to(sp_ref.at[1], lp_ref.at[1 - d], edge_send.at[d + 4], edge_recv.at[4 - d], lat + d, right),
        )

    @pl.when(top)
    def _():
        for i in range(NLON):
            pl.when(i != lon)(lambda i=i: first_copy(i).start())

    for d in (-1, 0, 1):
        def go(d=d):
            edge[d][0].start()
            edge[d][1].start()
        when(has[d], go)
    pl.when(has[1])(lambda: up.start())
    pl.when(has[-1])(lambda: down.start())

    for r in range(2, HROWS - 2):
        if r not in EARLY:
            hidden(r)
    loads[3].wait()
    for r in (2, 3, 4):
        output(r)

    @pl.when(top)
    def _():
        for half in (0, 1):
            at, n = HALF[half]

            @pl.when(my_half == half)
            def _():
                mine = x_ref.at[9 - my_row, pl.ds(at, n), pl.ds(pl.multiple_of(my_s * COLS, COLS), COLS)]
                a_ref[lon, 0:n] = mine[...]
                if n < 48:
                    a_ref[:, n:] = jnp.zeros((NLON, 48 - n, COLS), BF16)
                for e in range(NLON):
                    def arrive(e=e):
                        to(a_ref.at[e, pl.ds(0, n)], a_ref.at[e, pl.ds(0, n)], f1_send.at[e], f1_recv.at[e], lat, e).wait_recv()
                    pl.when(e != lon)(arrive)

        fold_kernel_parts(a_ref, y0_ref, y1_ref, s_ref, se_ref, fold_ref, lon)
        for half in (0, 1):
            at, n = HALF[half]

            @pl.when(my_half == half)
            def _():
                for d in range(NLON):
                    pl.when(d != lon)(lambda d=d: second_copy(d, half).start())
                x_ref[10 + my_row, at : at + n, pl.ds(pl.multiple_of(my_s * COLS, COLS), COLS)] = s_ref[lon, 0:n]
        for d in range(NLON):
            pl.when(d != lon)(lambda d=d: third_copy(d).start())
        fe_ref[lon] = se_ref[lon]

    output(5)

    @pl.when(top)
    def _():
        stack_taps(k1_raw, k1_pad, k1_ref, True)

    pl.when(has[-1])(lambda: up.wait_recv())
    shift_row(x_ref, xb_ref, 0)
    shift_row(x_ref, xb_ref, 1)
    hidden(1)
    hidden(0)
    output(1)
    output(0)

    for d in (-1, 0, 1):
        def got(d=d):
            edge[-d][0].wait_recv()
            edge[-d][1].wait_recv()
        when(has[d], got)
    pl.when(has[1])(lambda: down.wait_recv())

    @pl.when(top)
    def _():
        for e in range(NLON):
            row, s, half = piece(e)
            at, n = HALF[half]
            def arrive(e=e, row=row, s=s, at=at, n=n):
                there = x_ref.at[10 + row, pl.ds(at, n), pl.ds(s * COLS, COLS)]
                to(there, there, f2_send.at[e], f2_recv.at[e], lat, e).wait_recv()
                to(fe_ref.at[e], fe_ref.at[e], f3_send.at[e], f3_recv.at[e], lat, e).wait_recv()
            pl.when(e != lon)(arrive)
        for n, part in enumerate(fold_edges(fe_ref)):
            ft_ref[n] = part

    shift_row(x_ref, xb_ref, ROWS + 2)
    shift_row(x_ref, xb_ref, ROWS + 3)
    hidden(ROWS)
    hidden(ROWS + 1, jnp.where(top, 1, 0))
    output(6)
    output(7)

    pairs = edge_pairs(x_ref, (0, 1, 10, 11), pairs)
    lane = lanes_of((CPAD, 128))

    def joined(ref, n):
        below = pltpu.roll(ref[0].astype(F32), 64, 1)
        above = jnp.where(top, ft_ref[n], pltpu.roll(ref[2].astype(F32), 64, 1))
        return jnp.where(lane < 16, below, jnp.where(lane < 80, ref[1].astype(F32), above))

    before, after = joined(lp_ref, 0), joined(rp_ref, 1)
    even = jnp.bitwise_and(lane, 1) == 0
    columns = []
    for low, high in ((before, pairs[2]), (pairs[0], pairs[3]), (pairs[1], after)):
        columns.append(jnp.where(even, low, pltpu.roll(high, 1, 1)))
        columns.append(jnp.where(even, pltpu.roll(low, 127, 1), high))
    first, last = edge_columns(columns, k1_ref, k2_ref, bias1, bias2, top)
    edge_out[0] = first
    edge_out[1] = last

    pl.when(has[1])(lambda: up.wait_send())
    pl.when(has[-1])(lambda: down.wait_send())
    for d in (-1, 0, 1):
        def sent(d=d):
            edge[d][0].wait_send()
            edge[d][1].wait_send()
        when(has[d], sent)

    @pl.when(top)
    def _():
        for i in range(NLON):
            pl.when(i != lon)(lambda i=i: first_copy(i).wait_send())
        for half in (0, 1):
            @pl.when(my_half == half)
            def _():
                for d in range(NLON):
                    pl.when(d != lon)(lambda d=d: second_copy(d, half).wait_send())
        for d in range(NLON):
            pl.when(d != lon)(lambda d=d: third_copy(d).wait_send())
    for store in stores:
        store.wait()


HBM = pl.BlockSpec(memory_space=pl.ANY)


def main(state, mask, fold, k1, b1, k2, b2):
    dma = pltpu.SemaphoreType.DMA
    return pl.pallas_call(
        main_kernel,
        out_shape=(
            jax.ShapeDtypeStruct((SAMPLES, ROWS, HID, COLS), BF16),
            jax.ShapeDtypeStruct((2, HID, 128), F32),
        ),
        in_specs=[HBM, HBM, SMEM, HBM, VMEM, HBM, VMEM],
        out_specs=(HBM, VMEM),
        scratch_shapes=[
            pltpu.VMEM(state.shape, BF16),
            pltpu.VMEM(mask.shape, jnp.int32),
            pltpu.VMEM(k1.shape, BF16),
            pltpu.VMEM((9, HID, 128), F32),
            pltpu.VMEM((2, HID, 9 * CPAD), BF16),
            pltpu.VMEM(k2.shape, BF16),
            pltpu.VMEM((XROWS, CPAD, WIDE), BF16),
            pltpu.VMEM((SAMPLES, 2, CPAD * ROWS, 128), F32),
            pltpu.VMEM((XROWS, 3 * CPAD, WIDE), BF16),
            pltpu.VMEM((HROWS, 3 * HID, WIDE), BF16),
            pltpu.VMEM((ROWS, SAMPLES, HID, COLS), BF16),
            pltpu.VMEM((2, CPAD, 128), BF16),
            pltpu.VMEM((3, CPAD, 128), BF16),
            pltpu.VMEM((3, CPAD, 128), BF16),
            pltpu.VMEM((NLON, 48, COLS), BF16),
            pltpu.VMEM((NLON, 48, COLS), BF16),
            pltpu.VMEM((NLON, 48, COLS), BF16),
            pltpu.VMEM((NLON, 48, COLS), BF16),
            pltpu.VMEM((NLON, 16, 128), BF16),
            pltpu.VMEM((NLON, 16, 128), BF16),
            pltpu.VMEM((2, CPAD, 128), F32),
            dma((4,)), dma((ROWS,)),
            dma((2,)), dma((2,)), dma((6,)), dma((6,)),
            dma((NLON,)), dma((NLON,)), dma((NLON,)), dma((NLON,)), dma((NLON,)), dma((NLON,)),
        ],
        compiler_params=pltpu.CompilerParams(collective_id=0, has_side_effects=True, vmem_limit_bytes=LIMIT),
    )(state, mask, fold, k1, b1, k2, b2)


CHANNELS = 128


def order_kernel(y_ref, edge_ref, out_ref, t_ref):
    s = pl.program_id(0)
    lane = lanes_of((CHANNELS, 128))
    first = pltpu.roll(edge_ref[0], lax.rem(128 - 2 * s, 128), 1)
    last = pltpu.roll(edge_ref[1], lax.rem(126 - 2 * s, 128), 1)
    for r in range(ROWS):
        by = (128 - 8 * r) % 128
        low, high = (pltpu.roll(v, by, 1) if r else v for v in (first, last))
        t_ref[0, pl.ds(r, CHANNELS, stride=ROWS), :] = jnp.where(lane < 2, low, y_ref[0, r, :, :128].astype(F32))
        t_ref[1, pl.ds(r, CHANNELS, stride=ROWS), :] = jnp.where(lane >= 126, high, y_ref[0, r, :, 128:].astype(F32))
    for h in range(2):
        out_ref[0, :, :, h * 128 : (h + 1) * 128] = t_ref[h].reshape(CHANNELS, ROWS, 128).astype(BF16)


def order(y, edges):
    return pl.pallas_call(
        order_kernel,
        grid=(SAMPLES, HID // CHANNELS),
        out_shape=jax.ShapeDtypeStruct((SAMPLES, HID, ROWS, COLS), BF16),
        in_specs=[
            pl.BlockSpec((1, ROWS, CHANNELS, COLS), lambda s, c: (s, 0, c, 0)),
            pl.BlockSpec((2, CHANNELS, 128), lambda s, c: (0, c, 0)),
        ],
        out_specs=pl.BlockSpec((1, CHANNELS, ROWS, COLS), lambda s, c: (s, c, 0, 0)),
        scratch_shapes=[pltpu.VMEM((2, CHANNELS * ROWS, 128), F32)],
        compiler_params=pltpu.CompilerParams(vmem_limit_bytes=LIMIT),
    )(y, edges)


def on_device(state, mask, fold, first_kernel, first_bias, second_kernel, second_bias):
    y, edges = main(state, mask, fold, first_kernel, first_bias[None], second_kernel, second_bias[None])
    return order(y, edges)


def solution(mesh):
    return jax.shard_map(
        on_device,
        mesh=mesh,
        in_specs=(P(None, None, "lat", "lon"), P(None, "lat", "lon"), P("lon"), P(), P(), P(), P()),
        out_specs=P(None, None, "lat", "lon"),
        check_vma=False,
    )
```

time: 62 us -> 51.3 us (0.83)
  Pallas kernels: 59.5 us -> 48.6 us
    pallas_call x2, Pallas kernels: 59.5 us -> 48.6 us  [the longest x1 40.3 us: main(): pl.pallas_call(main_kernel, out_shape=(jax.ShapeDtypeStruct((SAMPLES, ROW...]
    unnamed x0 -> x1, local copies, waits for them, and re-layouts: none -> 2.07 us
    reshape x1 -> x0, local copies, waits for them, and re-layouts: 1.16 us -> none  [on_device(): k1 = jnp.transpose(both, (0, 2, 1, 3)).reshape(2, HID, 9 * CPAD)]
    another operation x2 -> x0, local copies, waits for them, and re-layouts: 1.06 us -> none  [on_device(): both = jnp.stack([taps, taps[::-1]])]
where the time goes in v2:
time: 51.3 us; the launch traced here: 50.7 us
  Pallas kernels  48.6 us (95%)
  local copies, waits for them, and re-layouts  2.07 us (4%)
    pallas_call x1, Pallas kernels, main(): pl.pallas_call(main_kernel, out_shape=(jax.ShapeDtypeStruct((SAMPLES, ROW...  40.3 us
    pallas_call x1, Pallas kernels, order(): pl.pallas_call(order_kernel, grid=(SAMPLES, HID // CHANNELS), out_shape=j...  8.3 us
    unnamed x1, local copies, waits for them, and re-layouts  2.07 us

profile of v2, /device:TPU:14, one launch (start us, length us, event | category | flops | bytes accessed | tf_op | source)
XLA Modules:
  0.0 50.7 jit_solution(7671002157425463949)
XLA Ops:
  0.0 2.1 %copy.8.k1_hbm = bf16[9,256,75]{2,1,0:T(8,128)(2,1)} copy(bf16[9,256,75]{1,2,0:T(8,128)(2,1)} %param.10) | data formatting | bytes 691200 | tf_op args[3]
  2.1 40.3 %shard_map.73 = (bf16[4,8,256,256]{3,2,1,0:T(8,128)(2,1)}, f32[2,256,128]{2,1,0:T(8,128)}) custom-call(bf16[4,75,8,256]{3,2,1,0:T(8,128)(2,1)} %state_hbm.1, s32[75,8,256]{2,1,0:T(8,128)} %mask_hbm.1, s32[256]{0:T(256)} %fold_ref.1, bf16[9,256,75]{2,1,0:T(8,128)(2,1)} %copy.8.k1_hbm, f32[1,256]{1,0:T(1,128)} %bitcast.2, bf16[9,256,256]{2,1,0:T(8,128)(2,1)} %k2_hbm.1, ...), custom_call_target="tpu_custom_call" | custom-call | tf_op jit(solution)/shard_map/pallas_call | solution.py:449
  42.4 8.3 %shard_map.74 = bf16[4,256,8,256]{3,2,1,0:T(8,128)(2,1)} custom-call(bf16[4,8,256,256]{3,2,1,0:T(8,128)(2,1)} %get-tuple-element.7.y_ref, f32[2,256,128]{2,1,0:T(8,128)} %get-tuple-element.8.edge_ref), custom_call_target="tpu_custom_call" | custom-call | tf_op jit(solution)/shard_map/pallas_call | solution.py:505

commit v3 on v2

--- a/solution.py
+++ b/solution.py
@@ -45,7 +45,8 @@
         for h in range(2):
             cut = slice(h * 128, (h + 1) * 128)
             t_ref[s, h, CIN * ROWS : (CIN + 1) * ROWS, :] = mask_ref[0, :, cut].astype(F32)
-            t_ref[s, h, (CIN + 1) * ROWS :, :] = jnp.zeros(((CPAD - CIN - 1) * ROWS, 128), F32)
+            t_ref[s, h, (CIN + 1) * ROWS : (CIN + 4) * ROWS, :] = jnp.ones((3 * ROWS, 128), F32)
+            t_ref[s, h, (CIN + 4) * ROWS :, :] = jnp.zeros(((CPAD - CIN - 4) * ROWS, 128), F32)
             masked = state_ref[s, :, :, cut].astype(F32) * mask_ref[:, :, cut].astype(F32)
             t_ref[s, h, : CIN * ROWS, :] = masked.reshape(CIN * ROWS, 128)
             for r in range(ROWS):
@@ -61,67 +62,66 @@
 EARLY = (2, 3, 4, 5)
 
 
-def gelu(x):
-    return 0.5 * x * (1.0 + jnp.tanh(0.7978845608028654 * (x + 0.044715 * (x * x * x))))
+def gelu_times(x, half_surface):
+    half = x * half_surface
+    return half + half * jnp.tanh(x * (0.7978845608028654 + 0.035677408136300125 * (x * x)))
 
 
 def wide_bias(ref):
     return jnp.transpose(jnp.broadcast_to(ref[...], (128, HID)))
 
 
-def stack_taps(raw_ref, pad_ref, k1_ref, turned):
-    lane = lanes_of((HID, 128))
-    blocks = [None] * 6
+def stack_taps(raw_ref, bias_ref, pad_ref, k1_ref, turned):
+    pad_ref[9 * CPAD :, :] = jnp.zeros((pad_ref.shape[0] - 9 * CPAD, HID), F32)
     for t in range(9):
-        if not turned:
-            pad_ref[t, :, CIN:] = jnp.zeros((HID, 128 - CIN), F32)
-            pad_ref[t, :, :CIN] = raw_ref[t].astype(F32)
         at = CPAD * (8 - t if turned else t)
-        q, p = at // 128, at % 128
-        moved = pltpu.roll(pad_ref[t], p, 1) if p else pad_ref[t]
-        for block, keep in ((q, lane >= p), (q + 1, lane < p)):
-            if block == q + 1 and p + CIN <= 128:
-                continue
-            part = jnp.where(keep, moved, 0.0)
-            blocks[block] = part if blocks[block] is None else blocks[block] + part
-    for n, block in enumerate(blocks):
-        wide = min(128, 9 * CPAD - n * 128)
-        k1_ref[1 if turned else 0, :, n * 128 : n * 128 + wide] = block[:, :wide].astype(BF16)
+        pad_ref[at + 72 : at + CPAD, :] = jnp.zeros((8, HID), F32)
+        pad_ref[at : at + CIN, :] = raw_ref[t].astype(F32)
+    at = 4 * CPAD + CIN + 1
+    rest = bias_ref[...]
+    for n in range(3):
+        part = rest.astype(BF16).astype(F32)
+        pad_ref[at + n : at + n + 1, :] = part
+        rest = rest - part
+    k1_ref[1 if turned else 0] = jnp.transpose(pad_ref[...])[:, : 9 * CPAD].astype(BF16)
 
 
 def shift_row(x_ref, xb_ref, r):
-    row = x_ref[r].astype(F32)
-    xb_ref[r, :CPAD, :] = pltpu.roll(row, 1, 1).astype(BF16)
-    xb_ref[r, CPAD : 2 * CPAD, :] = x_ref[r]
-    xb_ref[r, 2 * CPAD :, :] = pltpu.roll(row, WIDE - 1, 1).astype(BF16)
-
-
-def hidden_row(x_ref, xb_ref, hb_ref, k1_ref, bias, which, r):
+    row = x_ref[r]
+    xb_ref[r, :CPAD, :] = pltpu.roll(row, 1, 1)
+    xb_ref[r, CPAD : 2 * CPAD, :] = row
+    xb_ref[r, 2 * CPAD :, :] = pltpu.roll(row, WIDE - 1, 1)
+
+
+def hidden_row(x_ref, xb_ref, hb_ref, k1_ref, which, r):
     kernel = k1_ref[which]
     taps = xb_ref[r : r + 3].reshape(9 * CPAD, WIDE)
     for pair in range(2):
         cut = slice(pair * 2 * COLS, (pair + 1) * 2 * COLS)
         out = jnp.dot(kernel, taps[:, cut], preferred_element_type=F32)
         surface = x_ref[r + 1, 64:CPAD, cut].astype(F32)[CIN - 64 : CIN - 63]
-        out = gelu(out + jnp.concatenate([bias] * 4, 1)) * surface
-        hb_ref[r, :HID, cut] = pltpu.roll(out, 1, 1).astype(BF16)
-        hb_ref[r, HID : 2 * HID, cut] = out.astype(BF16)
-        hb_ref[r, 2 * HID :, cut] = pltpu.roll(out, 2 * COLS - 1, 1).astype(BF16)
+        out = gelu_times(out, 0.5 * surface).astype(BF16)
+        hb_ref[r, :HID, cut] = pltpu.roll(out, 1, 1)
+        hb_ref[r, HID : 2 * HID, cut] = out
+        hb_ref[r, 2 * HID :, cut] = pltpu.roll(out, 2 * COLS - 1, 1)
 
 
 def output_row(x_ref, hb_ref, k2_ref, y_ref, bias, r):
     kernel = jnp.concatenate([k2_ref[t] for t in range(9)], 1)
     taps = hb_ref[r : r + 3].reshape(9 * HID, WIDE)
+    column = jnp.bitwise_and(lanes_of((1, 2 * COLS)), COLS - 1)
+    inner = jnp.logical_and(column >= 2, column < COLS - 2)
     for pair in range(2):
         cut = slice(pair * 2 * COLS, (pair + 1) * 2 * COLS)
         out = jnp.dot(kernel, taps[:, cut], preferred_element_type=F32)
         surface = x_ref[r + 2, 64:CPAD, cut].astype(F32)[CIN - 64 : CIN - 63]
+        surface = jnp.where(inner, surface, 0.0)
         out = ((out + jnp.concatenate([bias] * 4, 1)) * surface).astype(BF16)
         y_ref[r, 2 * pair] = out[:, :COLS]
         y_ref[r, 2 * pair + 1] = out[:, COLS:]
 
 
-def edge_columns(columns, k1_ref, k2_ref, bias1, bias2, top):
+def edge_columns(columns, k1_ref, k2_ref, bias2, top):
     lane = lanes_of((HID, 128))
     back = [[c if not a else pltpu.roll(c, 128 - 8 * a, 1) for a in range(3)] for c in columns]
     taps = jnp.concatenate(
@@ -133,8 +133,8 @@
     hidden = []
     for i in range(4):
         cut = slice(i * 128, (i + 1) * 128)
-        out = jnp.where(ghost, turned[:, cut], plain[:, cut]) + bias1
-        out = gelu(out) * back[i + 1][1][CIN : CIN + 1, :]
+        out = jnp.where(ghost, turned[:, cut], plain[:, cut])
+        out = gelu_times(out, 0.5 * back[i + 1][1][CIN : CIN + 1, :])
         hidden.append([out if not a else pltpu.roll(out, 128 - 8 * a, 1) for a in range(3)])
     taps = jnp.concatenate(
         [jnp.concatenate([hidden[i + b][a] for a in range(3) for b in range(3)], 0).astype(BF16) for i in range(2)], 1
@@ -238,11 +238,11 @@
     sp_ref[0] = pairs[0].astype(BF16)
     sp_ref[1] = pairs[3].astype(BF16)
     loads[2].wait()
-    stack_taps(k1_raw, k1_pad, k1_ref, False)
-    bias1, bias2 = wide_bias(b1_ref), wide_bias(b2_ref)
+    stack_taps(k1_raw, b1_ref, k1_pad, k1_ref, False)
+    bias2 = wide_bias(b2_ref)
 
     def hidden(r, which=0):
-        hidden_row(x_ref, xb_ref, hb_ref, k1_ref, bias1, which, r)
+        hidden_row(x_ref, xb_ref, hb_ref, k1_ref, which, r)
 
     stores = []
 
@@ -315,11 +315,6 @@
         for i in range(NLON):
             pl.when(i != lon)(lambda i=i: first_copy(i).start())
 
-    for d in (-1, 0, 1):
-        def go(d=d):
-            edge[d][0].start()
-            edge[d][1].start()
-        when(has[d], go)
     pl.when(has[1])(lambda: up.start())
     pl.when(has[-1])(lambda: down.start())
 
@@ -359,11 +354,17 @@
             pl.when(d != lon)(lambda d=d: third_copy(d).start())
         fe_ref[lon] = se_ref[lon]
 
+    for d in (-1, 0, 1):
+        def go(d=d):
+            edge[d][0].start()
+            edge[d][1].start()
+        when(has[d], go)
+
     output(5)
 
     @pl.when(top)
     def _():
-        stack_taps(k1_raw, k1_pad, k1_ref, True)
+        stack_taps(k1_raw, b1_ref, k1_pad, k1_ref, True)
 
     pl.when(has[-1])(lambda: up.wait_recv())
     shift_row(x_ref, xb_ref, 0)
@@ -414,7 +415,7 @@
     for low, high in ((before, pairs[2]), (pairs[0], pairs[3]), (pairs[1], after)):
         columns.append(jnp.where(even, low, pltpu.roll(high, 1, 1)))
         columns.append(jnp.where(even, pltpu.roll(low, 127, 1), high))
-    first, last = edge_columns(columns, k1_ref, k2_ref, bias1, bias2, top)
+    first, last = edge_columns(columns, k1_ref, k2_ref, bias2, top)
     edge_out[0] = first
     edge_out[1] = last
 
@@ -458,7 +459,7 @@
             pltpu.VMEM(state.shape, BF16),
             pltpu.VMEM(mask.shape, jnp.int32),
             pltpu.VMEM(k1.shape, BF16),
-            pltpu.VMEM((9, HID, 128), F32),
+            pltpu.VMEM((6 * 128, HID), F32),
             pltpu.VMEM((2, HID, 9 * CPAD), BF16),
             pltpu.VMEM(k2.shape, BF16),
             pltpu.VMEM((XROWS, CPAD, WIDE), BF16),
@@ -485,39 +486,52 @@
 
 
 CHANNELS = 128
-
-
-def order_kernel(y_ref, edge_ref, out_ref, t_ref):
-    s = pl.program_id(0)
+CHUNKS = [(s, c) for s in range(SAMPLES) for c in range(HID // CHANNELS)]
+
+
+def order_kernel(y_hbm, edge_ref, out_hbm, y_ref, out_ref, load_sem, store_sem):
+    loads, stores = [], []
+    for n, (s, c) in enumerate(CHUNKS):
+        part = pl.ds(c * CHANNELS, CHANNELS)
+        loads.append(pltpu.make_async_copy(y_hbm.at[s, :, part], y_ref.at[n], load_sem.at[n]))
+        stores.append(pltpu.make_async_copy(out_ref.at[n], out_hbm.at[s, part], store_sem.at[n]))
+    for load in loads:
+        load.start()
     lane = lanes_of((CHANNELS, 128))
-    first = pltpu.roll(edge_ref[0], lax.rem(128 - 2 * s, 128), 1)
-    last = pltpu.roll(edge_ref[1], lax.rem(126 - 2 * s, 128), 1)
-    for r in range(ROWS):
-        by = (128 - 8 * r) % 128
-        low, high = (pltpu.roll(v, by, 1) if r else v for v in (first, last))
-        t_ref[0, pl.ds(r, CHANNELS, stride=ROWS), :] = jnp.where(lane < 2, low, y_ref[0, r, :, :128].astype(F32))
-        t_ref[1, pl.ds(r, CHANNELS, stride=ROWS), :] = jnp.where(lane >= 126, high, y_ref[0, r, :, 128:].astype(F32))
-    for h in range(2):
-        out_ref[0, :, :, h * 128 : (h + 1) * 128] = t_ref[h].reshape(CHANNELS, ROWS, 128).astype(BF16)
+    for n, (s, c) in enumerate(CHUNKS):
+        cut = slice(c * CHANNELS, (c + 1) * CHANNELS)
+        first, last = edge_ref[0, cut], edge_ref[1, cut]
+        loads[n].wait()
+        for r in range(ROWS):
+            at = 8 * r + 2 * s
+            low = jnp.where(lane < 2, pltpu.roll(first, (128 - at) % 128, 1), 0.0)
+            high = jnp.where(lane >= 126, pltpu.roll(last, (126 - at) % 128, 1), 0.0)
+            y_ref[n, r, :, :128] = y_ref[n, r, :, :128] + low.astype(BF16)
+            y_ref[n, r, :, 128:] = y_ref[n, r, :, 128:] + high.astype(BF16)
+        out_ref[n] = jnp.swapaxes(y_ref[n], 0, 1)
+        stores[n].start()
+    for store in stores:
+        store.wait()
 
 
 def order(y, edges):
     return pl.pallas_call(
         order_kernel,
-        grid=(SAMPLES, HID // CHANNELS),
         out_shape=jax.ShapeDtypeStruct((SAMPLES, HID, ROWS, COLS), BF16),
-        in_specs=[
-            pl.BlockSpec((1, ROWS, CHANNELS, COLS), lambda s, c: (s, 0, c, 0)),
-            pl.BlockSpec((2, CHANNELS, 128), lambda s, c: (0, c, 0)),
+        in_specs=[HBM, VMEM],
+        out_specs=HBM,
+        scratch_shapes=[
+            pltpu.VMEM((len(CHUNKS), ROWS, CHANNELS, COLS), BF16),
+            pltpu.VMEM((len(CHUNKS), CHANNELS, ROWS, COLS), BF16),
+            pltpu.SemaphoreType.DMA((len(CHUNKS),)),
+            pltpu.SemaphoreType.DMA((len(CHUNKS),)),
         ],
-        out_specs=pl.BlockSpec((1, CHANNELS, ROWS, COLS), lambda s, c: (s, c, 0, 0)),
-        scratch_shapes=[pltpu.VMEM((2, CHANNELS * ROWS, 128), F32)],
         compiler_params=pltpu.CompilerParams(vmem_limit_bytes=LIMIT),
     )(y, edges)
 
 
 def on_device(state, mask, fold, first_kernel, first_bias, second_kernel, second_bias):
-    y, edges = main(state, mask, fold, first_kernel, first_bias[None], second_kernel, second_bias[None])
+    y, edges = main(state, mask, fold, jnp.transpose(first_kernel, (0, 2, 1)), first_bias[None], second_kernel, second_bias[None])
     return order(y, edges)
 
 

time: 51.3 us -> 45.1 us (0.88)
  Pallas kernels: 48.6 us -> 44.5 us
  local copies, waits for them, and re-layouts: 2.07 us -> 0 us
    pallas_call x1, Pallas kernels: 8.3 us -> 5.68 us  [order(): pl.pallas_call(order_kernel, out_shape=jax.ShapeDtypeStruct((SAMPLES, HID...]
    unnamed x1 -> x0, local copies, waits for them, and re-layouts: 2.07 us -> none
    pallas_call x1, Pallas kernels: 40.3 us -> 38.8 us  [main(): pl.pallas_call(main_kernel, out_shape=(jax.ShapeDtypeStruct((SAMPLES, ROW...]
where the time goes in v3:
time: 45.1 us; the launch traced here: 44.6 us
  Pallas kernels  44.5 us (99%)
    pallas_call x1, Pallas kernels, main(): pl.pallas_call(main_kernel, out_shape=(jax.ShapeDtypeStruct((SAMPLES, ROW...  38.8 us
    pallas_call x1, Pallas kernels, order(): pl.pallas_call(order_kernel, out_shape=jax.ShapeDtypeStruct((SAMPLES, HID...  5.68 us

profile of v3, /device:TPU:14, one launch (start us, length us, event | category | flops | bytes accessed | tf_op | source)
XLA Modules:
  0.0 44.6 jit_solution(2393681088123441797)
XLA Ops:
  0.0 38.8 %shard_map.73 = (bf16[4,8,256,256]{3,2,1,0:T(8,128)(2,1)}, f32[2,256,128]{2,1,0:T(8,128)}) custom-call(bf16[4,75,8,256]{3,2,1,0:T(8,128)(2,1)} %state_hbm.1, s32[75,8,256]{2,1,0:T(8,128)} %mask_hbm.1, s32[256]{0:T(256)} %fold_ref.1, bf16[9,75,256]{2,1,0:T(8,128)(2,1)} %bitcast.3, f32[1,256]{1,0:T(1,128)} %bitcast.4, bf16[9,256,256]{2,1,0:T(8,128)(2,1)} %k2_hbm.1, ...), custom_call_target="tpu_custom_call" | custom-call | tf_op jit(solution)/shard_map/pallas_call | solution.py:450
  38.8 5.7 %shard_map.74 = bf16[4,256,8,256]{3,2,1,0:T(8,128)(2,1)} custom-call(bf16[4,8,256,256]{3,2,1,0:T(8,128)(2,1)} %get-tuple-element.7.y_hbm, f32[2,256,128]{2,1,0:T(8,128)} %get-tuple-element.8.edge_ref), custom_call_target="tpu_custom_call" | custom-call | tf_op jit(solution)/shard_map/pallas_call | solution.py:518

commit v4 on v3

--- a/solution.py
+++ b/solution.py
@@ -191,9 +191,9 @@
 def main_kernel(
     state_hbm, mask_hbm, fold_ref, k1_hbm, b1_ref, k2_hbm, b2_ref, y_hbm, edge_out,
     state_ref, mask_ref, k1_raw, k1_pad, k1_ref, k2_ref, x_ref, t_ref, xb_ref, hb_ref, y_ref,
-    sp_ref, lp_ref, rp_ref, a_ref, y0_ref, y1_ref, s_ref, se_ref, fe_ref, ft_ref,
+    sp_ref, lp_ref, rp_ref, relay_ref, a_ref, y0_ref, y1_ref, s_ref, se_ref, fe_ref, ft_ref,
     load_sem, store_sem,
-    row_send, row_recv, edge_send, edge_recv, f1_send, f1_recv, f2_send, f2_recv, f3_send, f3_recv,
+    row_send, row_recv, relay_send, relay_recv, pass_send, pass_recv, edge_send, edge_recv, f1_send, f1_recv, f2_send, f2_recv, f3_send, f3_recv,
 ):
     loads = [
         pltpu.make_async_copy(src, dst, load_sem.at[n])
@@ -231,12 +231,16 @@
         for k in range(2, NLON - 1):
             greet(lat, lax.rem(lon + k, NLON))
 
+    is_relay, is_low, is_high = lat == 0, lat == NLAT // 2 - 1, lat == NLAT // 2
+    pl.when(is_relay)(lambda: [greet(NLAT // 2 - 1, lon), greet(NLAT // 2, lon)] and None)
+    pl.when(jnp.logical_or(is_low, is_high))(lambda: greet(0, lon))
+
     loads[0].wait()
     loads[1].wait()
     prepare(state_ref, mask_ref, x_ref, t_ref)
     pairs = edge_pairs(x_ref, range(2, 2 + ROWS), [jnp.zeros((CPAD, 128), F32)] * 4)
-    sp_ref[0] = pairs[0].astype(BF16)
-    sp_ref[1] = pairs[3].astype(BF16)
+    for n, pair in enumerate((pairs[0], pairs[3])):
+        sp_ref[n] = jnp.transpose(jnp.concatenate([pair, jnp.zeros((48, 128), F32)], 0)).astype(BF16)
     loads[2].wait()
     stack_taps(k1_raw, b1_ref, k1_pad, k1_ref, False)
     bias2 = wide_bias(b2_ref)
@@ -259,16 +263,20 @@
     @pl.when(lat == 0)
     def _():
         x_ref[0:2] = jnp.zeros((2, CPAD, WIDE), BF16)
-        lp_ref[0] = jnp.zeros((CPAD, 128), BF16)
-        rp_ref[0] = jnp.zeros((CPAD, 128), BF16)
-
-    @pl.when(jnp.logical_and(lat > 0, lat < NLAT - 1))
+        lp_ref[0:16] = jnp.zeros((16, 128), BF16)
+        rp_ref[0:16] = jnp.zeros((16, 128), BF16)
+
+    @pl.when(jnp.logical_or(is_low, is_high))
+    def _():
+        pl.semaphore_wait(barrier, 9)
+
+    @pl.when(jnp.logical_and(jnp.logical_and(lat > 0, lat < NLAT - 1), jnp.logical_not(jnp.logical_or(is_low, is_high))))
     def _():
         pl.semaphore_wait(barrier, 8)
 
     @pl.when(lat == 0)
     def _():
-        pl.semaphore_wait(barrier, 5)
+        pl.semaphore_wait(barrier, 7)
 
     @pl.when(top)
     def _():
@@ -302,12 +310,31 @@
         return to(se_ref.at[d], fe_ref.at[lon], f3_send.at[d], f3_recv.at[lon], lat, d)
 
     up = to(x_ref.at[pl.ds(8, 2)], x_ref.at[pl.ds(0, 2)], row_send.at[0], row_recv.at[0], lat + 1, lon)
+    def relay_copy(s):
+        return to(
+            x_ref.at[pl.ds(2, 2), :, pl.ds(s * COLS, COLS)], relay_ref.at[s],
+            relay_send.at[s], relay_recv.at[s], 0, lon,
+        )
+
+    def pass_copy(s):
+        return to(
+            relay_ref.at[s], x_ref.at[pl.ds(10, 2), :, pl.ds(s * COLS, COLS)],
+            pass_send.at[s], pass_recv.at[s], NLAT // 2 - 1, lon,
+        )
+
+    def hand_on(s):
+        @pl.when(is_relay)
+        def _():
+            relay_copy(s).wait_recv()
+            pass_copy(s).start()
+
+    direct = jnp.logical_and(lat > 0, jnp.logical_not(is_high))
     down = to(x_ref.at[pl.ds(2, 2)], x_ref.at[pl.ds(10, 2)], row_send.at[1], row_recv.at[1], lat - 1, lon)
     edge = {}
-    for d in (-1, 0, 1):
+    for d, at, n, there in ((-1, 16, 16, 80), (0, 16, 64, 16), (1, 64, 16, 0)):
         edge[d] = (
-            to(sp_ref.at[0], rp_ref.at[1 - d], edge_send.at[d + 1], edge_recv.at[1 - d], lat + d, left),
-            to(sp_ref.at[1], lp_ref.at[1 - d], edge_send.at[d + 4], edge_recv.at[4 - d], lat + d, right),
+            to(sp_ref.at[0, pl.ds(at, n)], rp_ref.at[pl.ds(there, n)], edge_send.at[d + 1], edge_recv.at[1 - d], lat + d, left),
+            to(sp_ref.at[1, pl.ds(at, n)], lp_ref.at[pl.ds(there, n)], edge_send.at[d + 4], edge_recv.at[4 - d], lat + d, right),
         )
 
     @pl.when(top)
@@ -315,15 +342,28 @@
         for i in range(NLON):
             pl.when(i != lon)(lambda i=i: first_copy(i).start())
 
+    for d in (-1, 0, 1):
+        def go(d=d):
+            edge[d][0].start()
+            edge[d][1].start()
+        when(has[d], go)
+    @pl.when(is_high)
+    def _():
+        for s in range(SAMPLES):
+            relay_copy(s).start()
+
     pl.when(has[1])(lambda: up.start())
-    pl.when(has[-1])(lambda: down.start())
+    pl.when(direct)(lambda: down.start())
 
     for r in range(2, HROWS - 2):
         if r not in EARLY:
             hidden(r)
     loads[3].wait()
-    for r in (2, 3, 4):
-        output(r)
+    output(2)
+    output(3)
+    hand_on(0)
+    output(4)
+    hand_on(1)
 
     @pl.when(top)
     def _():
@@ -354,13 +394,8 @@
             pl.when(d != lon)(lambda d=d: third_copy(d).start())
         fe_ref[lon] = se_ref[lon]
 
-    for d in (-1, 0, 1):
-        def go(d=d):
-            edge[d][0].start()
-            edge[d][1].start()
-        when(has[d], go)
-
     output(5)
+    hand_on(2)
 
     @pl.when(top)
     def _():
@@ -371,15 +406,16 @@
     shift_row(x_ref, xb_ref, 1)
     hidden(1)
     hidden(0)
+    hand_on(3)
     output(1)
     output(0)
 
-    for d in (-1, 0, 1):
-        def got(d=d):
-            edge[-d][0].wait_recv()
-            edge[-d][1].wait_recv()
-        when(has[d], got)
-    pl.when(has[1])(lambda: down.wait_recv())
+    pl.when(jnp.logical_and(has[1], jnp.logical_not(is_low)))(lambda: down.wait_recv())
+
+    @pl.when(is_low)
+    def _():
+        for s in range(SAMPLES):
+            pass_copy(s).wait_recv()
 
     @pl.when(top)
     def _():
@@ -401,13 +437,17 @@
     output(6)
     output(7)
 
+    for d in (-1, 0, 1):
+        def got(d=d):
+            edge[-d][0].wait_recv()
+            edge[-d][1].wait_recv()
+        when(has[d], got)
     pairs = edge_pairs(x_ref, (0, 1, 10, 11), pairs)
     lane = lanes_of((CPAD, 128))
 
     def joined(ref, n):
-        below = pltpu.roll(ref[0].astype(F32), 64, 1)
-        above = jnp.where(top, ft_ref[n], pltpu.roll(ref[2].astype(F32), 64, 1))
-        return jnp.where(lane < 16, below, jnp.where(lane < 80, ref[1].astype(F32), above))
+        sent = jnp.transpose(ref[...].astype(F32))[:CPAD]
+        return jnp.where(jnp.logical_and(top, lane >= 80), ft_ref[n], sent)
 
     before, after = joined(lp_ref, 0), joined(rp_ref, 1)
     even = jnp.bitwise_and(lane, 1) == 0
@@ -416,11 +456,23 @@
         columns.append(jnp.where(even, low, pltpu.roll(high, 1, 1)))
         columns.append(jnp.where(even, pltpu.roll(low, 127, 1), high))
     first, last = edge_columns(columns, k1_ref, k2_ref, bias2, top)
-    edge_out[0] = first
-    edge_out[1] = last
+    used = lanes_of((HID, 128)) < 64
+    edge_out[0] = jnp.where(used, first, 0.0).astype(BF16)
+    edge_out[1] = jnp.where(used, last, 0.0).astype(BF16)
 
     pl.when(has[1])(lambda: up.wait_send())
-    pl.when(has[-1])(lambda: down.wait_send())
+    pl.when(direct)(lambda: down.wait_send())
+
+    @pl.when(is_high)
+    def _():
+        for s in range(SAMPLES):
+            relay_copy(s).wait_send()
+
+    @pl.when(is_relay)
+    def _():
+        for s in range(SAMPLES):
+            pass_copy(s).wait_send()
+
     for d in (-1, 0, 1):
         def sent(d=d):
             edge[d][0].wait_send()
@@ -451,7 +503,7 @@
         main_kernel,
         out_shape=(
             jax.ShapeDtypeStruct((SAMPLES, ROWS, HID, COLS), BF16),
-            jax.ShapeDtypeStruct((2, HID, 128), F32),
+            jax.ShapeDtypeStruct((2, HID, 128), BF16),
         ),
         in_specs=[HBM, HBM, SMEM, HBM, VMEM, HBM, VMEM],
         out_specs=(HBM, VMEM),
@@ -467,9 +519,10 @@
             pltpu.VMEM((XROWS, 3 * CPAD, WIDE), BF16),
             pltpu.VMEM((HROWS, 3 * HID, WIDE), BF16),
             pltpu.VMEM((ROWS, SAMPLES, HID, COLS), BF16),
-            pltpu.VMEM((2, CPAD, 128), BF16),
-            pltpu.VMEM((3, CPAD, 128), BF16),
-            pltpu.VMEM((3, CPAD, 128), BF16),
+            pltpu.VMEM((2, 128, 128), BF16),
+            pltpu.VMEM((128, 128), BF16),
+            pltpu.VMEM((128, 128), BF16),
+            pltpu.VMEM((SAMPLES, 2, CPAD, COLS), BF16),
             pltpu.VMEM((NLON, 48, COLS), BF16),
             pltpu.VMEM((NLON, 48, COLS), BF16),
             pltpu.VMEM((NLON, 48, COLS), BF16),
@@ -478,7 +531,7 @@
             pltpu.VMEM((NLON, 16, 128), BF16),
             pltpu.VMEM((2, CPAD, 128), F32),
             dma((4,)), dma((ROWS,)),
-            dma((2,)), dma((2,)), dma((6,)), dma((6,)),
+            dma((2,)), dma((2,)), dma((SAMPLES,)), dma((SAMPLES,)), dma((SAMPLES,)), dma((SAMPLES,)), dma((6,)), dma((6,)),
             dma((NLON,)), dma((NLON,)), dma((NLON,)), dma((NLON,)), dma((NLON,)), dma((NLON,)),
         ],
         compiler_params=pltpu.CompilerParams(collective_id=0, has_side_effects=True, vmem_limit_bytes=LIMIT),
@@ -486,6 +539,7 @@
 
 
 CHANNELS = 128
+AHEAD = 8
 CHUNKS = [(s, c) for s in range(SAMPLES) for c in range(HID // CHANNELS)]
 
 
@@ -495,19 +549,23 @@
         part = pl.ds(c * CHANNELS, CHANNELS)
         loads.append(pltpu.make_async_copy(y_hbm.at[s, :, part], y_ref.at[n], load_sem.at[n]))
         stores.append(pltpu.make_async_copy(out_ref.at[n], out_hbm.at[s, part], store_sem.at[n]))
-    for load in loads:
+    for load in loads[:AHEAD]:
         load.start()
     lane = lanes_of((CHANNELS, 128))
+    at_first = jnp.where(lane < 2, 1.0, 0.0).astype(BF16)
+    at_last = jnp.where(lane >= 126, 1.0, 0.0).astype(BF16)
     for n, (s, c) in enumerate(CHUNKS):
         cut = slice(c * CHANNELS, (c + 1) * CHANNELS)
         first, last = edge_ref[0, cut], edge_ref[1, cut]
         loads[n].wait()
+        if n + AHEAD < len(loads):
+            loads[n + AHEAD].start()
         for r in range(ROWS):
             at = 8 * r + 2 * s
-            low = jnp.where(lane < 2, pltpu.roll(first, (128 - at) % 128, 1), 0.0)
-            high = jnp.where(lane >= 126, pltpu.roll(last, (126 - at) % 128, 1), 0.0)
-            y_ref[n, r, :, :128] = y_ref[n, r, :, :128] + low.astype(BF16)
-            y_ref[n, r, :, 128:] = y_ref[n, r, :, 128:] + high.astype(BF16)
+            low = at_first * (pltpu.roll(first, 128 - at, 1) if at else first)
+            high = at_last * pltpu.roll(last, 126 - at, 1)
+            y_ref[n, r, :, :128] = y_ref[n, r, :, :128] + low
+            y_ref[n, r, :, 128:] = y_ref[n, r, :, 128:] + high
         out_ref[n] = jnp.swapaxes(y_ref[n], 0, 1)
         stores[n].start()
     for store in stores:

time: 45.1 us -> 38.3 us (0.85)
  Pallas kernels: 44.5 us -> 37.7 us
    pallas_call x1, Pallas kernels: 38.8 us -> 32.2 us  [main(): pl.pallas_call(main_kernel, out_shape=(jax.ShapeDtypeStruct((SAMPLES, ROW...]
where the time goes in v4:
time: 38.3 us; the launch traced here: 37.9 us
  Pallas kernels  37.7 us (98%)
    pallas_call x1, Pallas kernels, main(): pl.pallas_call(main_kernel, out_shape=(jax.ShapeDtypeStruct((SAMPLES, ROW...  32.2 us
    pallas_call x1, Pallas kernels, order(): pl.pallas_call(order_kernel, out_shape=jax.ShapeDtypeStruct((SAMPLES, HID...  5.49 us

profile of v4, /device:TPU:14, one launch (start us, length us, event | category | flops | bytes accessed | tf_op | source)
XLA Modules:
  0.0 37.9 jit_solution(17501677814815378564)
XLA Ops:
  0.0 32.2 %shard_map.73 = (bf16[4,8,256,256]{3,2,1,0:T(8,128)(2,1)}, bf16[2,256,128]{2,1,0:T(8,128)(2,1)}) custom-call(bf16[4,75,8,256]{3,2,1,0:T(8,128)(2,1)} %state_hbm.1, s32[75,8,256]{2,1,0:T(8,128)} %mask_hbm.1, s32[256]{0:T(256)} %fold_ref.1, bf16[9,75,256]{2,1,0:T(8,128)(2,1)} %bitcast.3, f32[1,256]{1,0:T(1,128)} %bitcast.4, bf16[9,256,256]{2,1,0:T(8,128)(2,1)} %k2_hbm.1, ...), custom_call_target="tpu_custom_call" | custom-call | tf_op jit(solution)/shard_map/pallas_call | solution.py:502
  32.2 5.5 %shard_map.74 = bf16[4,256,8,256]{3,2,1,0:T(8,128)(2,1)} custom-call(bf16[4,8,256,256]{3,2,1,0:T(8,128)(2,1)} %get-tuple-element.7.y_hbm, bf16[2,256,128]{2,1,0:T(8,128)(2,1)} %get-tuple-element.8.edge_ref), custom_call_target="tpu_custom_call" | custom-call | tf_op jit(solution)/shard_map/pallas_call | solution.py:576

commit v5 on v4

--- a/solution.py
+++ b/solution.py
@@ -59,7 +59,6 @@
 
 
 HALF = ((0, 48), (48, 32))
-EARLY = (2, 3, 4, 5)
 
 
 def gelu_times(x, half_surface):
@@ -238,12 +237,6 @@
     loads[0].wait()
     loads[1].wait()
     prepare(state_ref, mask_ref, x_ref, t_ref)
-    pairs = edge_pairs(x_ref, range(2, 2 + ROWS), [jnp.zeros((CPAD, 128), F32)] * 4)
-    for n, pair in enumerate((pairs[0], pairs[3])):
-        sp_ref[n] = jnp.transpose(jnp.concatenate([pair, jnp.zeros((48, 128), F32)], 0)).astype(BF16)
-    loads[2].wait()
-    stack_taps(k1_raw, b1_ref, k1_pad, k1_ref, False)
-    bias2 = wide_bias(b2_ref)
 
     def hidden(r, which=0):
         hidden_row(x_ref, xb_ref, hb_ref, k1_ref, which, r)
@@ -254,11 +247,6 @@
         output_row(x_ref, hb_ref, k2_ref, y_ref, bias2, r)
         stores.append(pltpu.make_async_copy(y_ref.at[r], y_hbm.at[:, r], store_sem.at[r]))
         stores[-1].start()
-
-    for r in range(2, 2 + ROWS):
-        shift_row(x_ref, xb_ref, r)
-    for r in EARLY:
-        hidden(r)
 
     @pl.when(lat == 0)
     def _():
@@ -342,28 +330,31 @@
         for i in range(NLON):
             pl.when(i != lon)(lambda i=i: first_copy(i).start())
 
+    @pl.when(is_high)
+    def _():
+        for s in range(SAMPLES):
+            relay_copy(s).start()
+
+    pl.when(has[1])(lambda: up.start())
+    pl.when(direct)(lambda: down.start())
+    pairs = edge_pairs(x_ref, range(2, 2 + ROWS), [jnp.zeros((CPAD, 128), F32)] * 4)
+    for n, pair in enumerate((pairs[0], pairs[3])):
+        sp_ref[n] = jnp.transpose(jnp.concatenate([pair, jnp.zeros((48, 128), F32)], 0)).astype(BF16)
     for d in (-1, 0, 1):
         def go(d=d):
             edge[d][0].start()
             edge[d][1].start()
         when(has[d], go)
-    @pl.when(is_high)
-    def _():
-        for s in range(SAMPLES):
-            relay_copy(s).start()
-
-    pl.when(has[1])(lambda: up.start())
-    pl.when(direct)(lambda: down.start())
+    loads[2].wait()
+    stack_taps(k1_raw, b1_ref, k1_pad, k1_ref, False)
+    bias2 = wide_bias(b2_ref)
+    for r in range(2, 2 + ROWS):
+        shift_row(x_ref, xb_ref, r)
 
     for r in range(2, HROWS - 2):
-        if r not in EARLY:
-            hidden(r)
+        hidden(r)
     loads[3].wait()
     output(2)
-    output(3)
-    hand_on(0)
-    output(4)
-    hand_on(1)
 
     @pl.when(top)
     def _():
@@ -394,8 +385,12 @@
             pl.when(d != lon)(lambda d=d: third_copy(d).start())
         fe_ref[lon] = se_ref[lon]
 
+    hand_on(0)
+    output(3)
+    hand_on(1)
+    output(4)
+    hand_on(2)
     output(5)
-    hand_on(2)
 
     @pl.when(top)
     def _():
@@ -404,9 +399,9 @@
     pl.when(has[-1])(lambda: up.wait_recv())
     shift_row(x_ref, xb_ref, 0)
     shift_row(x_ref, xb_ref, 1)
+    hand_on(3)
     hidden(1)
     hidden(0)
-    hand_on(3)
     output(1)
     output(0)
 

time: 38.3 us -> 36.9 us (0.963)
  Pallas kernels: 37.7 us -> 36.3 us
    pallas_call x1, Pallas kernels: 32.2 us -> 30.8 us  [main(): pl.pallas_call(main_kernel, out_shape=(jax.ShapeDtypeStruct((SAMPLES, ROW...]
where the time goes in v5:
time: 36.9 us; the launch traced here: 36.5 us
  Pallas kernels  36.3 us (98%)
    pallas_call x1, Pallas kernels, main(): pl.pallas_call(main_kernel, out_shape=(jax.ShapeDtypeStruct((SAMPLES, ROW...  30.8 us
    pallas_call x1, Pallas kernels, order(): pl.pallas_call(order_kernel, out_shape=jax.ShapeDtypeStruct((SAMPLES, HID...  5.49 us

profile of v5, /device:TPU:14, one launch (start us, length us, event | category | flops | bytes accessed | tf_op | source)
XLA Modules:
  0.0 36.5 jit_solution(2193740439613322637)
XLA Ops:
  0.0 30.8 %shard_map.73 = (bf16[4,8,256,256]{3,2,1,0:T(8,128)(2,1)}, bf16[2,256,128]{2,1,0:T(8,128)(2,1)}) custom-call(bf16[4,75,8,256]{3,2,1,0:T(8,128)(2,1)} %state_hbm.1, s32[75,8,256]{2,1,0:T(8,128)} %mask_hbm.1, s32[256]{0:T(256)} %fold_ref.1, bf16[9,75,256]{2,1,0:T(8,128)(2,1)} %bitcast.3, f32[1,256]{1,0:T(1,128)} %bitcast.4, bf16[9,256,256]{2,1,0:T(8,128)(2,1)} %k2_hbm.1, ...), custom_call_target="tpu_custom_call" | custom-call | tf_op jit(solution)/shard_map/pallas_call | solution.py:497
  30.8 5.5 %shard_map.74 = bf16[4,256,8,256]{3,2,1,0:T(8,128)(2,1)} custom-call(bf16[4,8,256,256]{3,2,1,0:T(8,128)(2,1)} %get-tuple-element.7.y_hbm, bf16[2,256,128]{2,1,0:T(8,128)(2,1)} %get-tuple-element.8.edge_ref), custom_call_target="tpu_custom_call" | custom-call | tf_op jit(solution)/shard_map/pallas_call | solution.py:571

commit v6 on v5

--- a/solution.py
+++ b/solution.py
@@ -19,7 +19,8 @@
 XROWS = ROWS + 4
 HROWS = ROWS + 2
 NLON, NLAT = 16, 8
-LIMIT = 60 * 1024 * 1024
+MAIN_LIMIT = 44 * 1024 * 1024
+ORDER_LIMIT = 16 * 1024 * 1024
 
 
 def lanes_of(shape):
@@ -198,8 +199,8 @@
         pltpu.make_async_copy(src, dst, load_sem.at[n])
         for n, (src, dst) in enumerate(((mask_hbm, mask_ref), (state_hbm, state_ref), (k1_hbm, k1_raw), (k2_hbm, k2_ref)))
     ]
-    for load in loads:
-        load.start()
+    for n in (2, 0, 1, 3):
+        loads[n].start()
     lon = lax.axis_index("lon")
     lat = lax.axis_index("lat")
     right, left = lax.rem(lon + 1, NLON), lax.rem(lon + NLON - 1, NLON)
@@ -234,6 +235,9 @@
     pl.when(is_relay)(lambda: [greet(NLAT // 2 - 1, lon), greet(NLAT // 2, lon)] and None)
     pl.when(jnp.logical_or(is_low, is_high))(lambda: greet(0, lon))
 
+    loads[2].wait()
+    stack_taps(k1_raw, b1_ref, k1_pad, k1_ref, False)
+    bias2 = wide_bias(b2_ref)
     loads[0].wait()
     loads[1].wait()
     prepare(state_ref, mask_ref, x_ref, t_ref)
@@ -345,9 +349,6 @@
             edge[d][0].start()
             edge[d][1].start()
         when(has[d], go)
-    loads[2].wait()
-    stack_taps(k1_raw, b1_ref, k1_pad, k1_ref, False)
-    bias2 = wide_bias(b2_ref)
     for r in range(2, 2 + ROWS):
         shift_row(x_ref, xb_ref, r)
 
@@ -529,7 +530,7 @@
             dma((2,)), dma((2,)), dma((SAMPLES,)), dma((SAMPLES,)), dma((SAMPLES,)), dma((SAMPLES,)), dma((6,)), dma((6,)),
             dma((NLON,)), dma((NLON,)), dma((NLON,)), dma((NLON,)), dma((NLON,)), dma((NLON,)),
         ],
-        compiler_params=pltpu.CompilerParams(collective_id=0, has_side_effects=True, vmem_limit_bytes=LIMIT),
+        compiler_params=pltpu.CompilerParams(collective_id=0, has_side_effects=True, vmem_limit_bytes=MAIN_LIMIT),
     )(state, mask, fold, k1, b1, k2, b2)
 
 
@@ -579,7 +580,7 @@
             pltpu.SemaphoreType.DMA((len(CHUNKS),)),
             pltpu.SemaphoreType.DMA((len(CHUNKS),)),
         ],
-        compiler_params=pltpu.CompilerParams(vmem_limit_bytes=LIMIT),
+        compiler_params=pltpu.CompilerParams(vmem_limit_bytes=ORDER_LIMIT),
     )(y, edges)
 
 

time: 36.9 us -> 42.4 us (1.15)
  local copies, waits for them, and re-layouts: 0 us -> 6.65 us
  Pallas kernels: 36.3 us -> 35 us
    unnamed x0 -> x14, local copies, waits for them, and re-layouts: none -> 6.65 us
    pallas_call x1, Pallas kernels: 5.49 us -> 3.86 us  [order(): pl.pallas_call(order_kernel, out_shape=jax.ShapeDtypeStruct((SAMPLES, HID...]
where the time goes in v6:
time: 42.4 us; the launch traced here: 41.8 us
  Pallas kernels  35 us (83%)
  local copies, waits for them, and re-layouts  6.65 us (16%)
    pallas_call x1, Pallas kernels, main(): pl.pallas_call(main_kernel, out_shape=(jax.ShapeDtypeStruct((SAMPLES, ROW...  31.1 us
    unnamed x14, local copies, waits for them, and re-layouts  6.65 us
    pallas_call x1, Pallas kernels, order(): pl.pallas_call(order_kernel, out_shape=jax.ShapeDtypeStruct((SAMPLES, HID...  3.86 us

profile of v6, /device:TPU:14, one launch (start us, length us, event | category | flops | bytes accessed | tf_op | source)
XLA Modules:
  0.0 41.8 jit_solution(11045263945020488114)
XLA Ops:
  0.0 0.0 copy-start
  0.0 1.3 %copy-done = bf16[4,75,8,256]{3,2,1,0:T(8,128)(2,1)S(1)} copy-done((bf16[4,75,8,256]{3,2,1,0:T(8,128)(2,1)S(1)}, bf16[4,75,8,256]{3,2,1,0:T(8,128)(2,1)}, u32[]{:S(2)}) %copy-start) | copy-done | bytes 1228824
  1.3 0.0 copy-start.1
  1.3 1.3 %copy-done.1 = bf16[9,256,256]{2,1,0:T(8,128)(2,1)S(1)} copy-done((bf16[9,256,256]{2,1,0:T(8,128)(2,1)S(1)}, bf16[9,256,256]{2,1,0:T(8,128)(2,1)}, u32[]{:S(2)}) %copy-start.1) | copy-done | bytes 1179672
  2.6 0.0 copy-start.2
  2.6 1.1 %copy-done.2 = s32[75,8,256]{2,1,0:T(8,128)S(1)} copy-done((s32[75,8,256]{2,1,0:T(8,128)S(1)}, s32[75,8,256]{2,1,0:T(8,128)}, u32[]{:S(2)}) %copy-start.2) | copy-done | bytes 614424
  3.6 0.0 copy-start.3
  3.6 1.0 %copy-done.3 = bf16[9,256,75]{1,2,0:T(8,128)(2,1)S(1)} copy-done((bf16[9,256,75]{1,2,0:T(8,128)(2,1)S(1)}, bf16[9,256,75]{1,2,0:T(8,128)(2,1)}, u32[]{:S(2)}) %copy-start.3) | copy-done | bytes 345624
  4.6 0.0 copy-start.4
  4.6 0.7 %copy-done.4 = s32[256]{0:T(256)S(1)} copy-done((s32[256]{0:T(256)S(1)}, s32[256]{0:T(256)}, u32[]{:S(2)}) %copy-start.4) | copy-done | bytes 1048
  5.3 0.0 copy-start.5
  5.3 0.7 %copy-done.5 = f32[256]{0:T(256)S(1)} copy-done((f32[256]{0:T(256)S(1)}, f32[256]{0:T(256)}, u32[]{:S(2)}) %copy-start.5) | copy-done | bytes 1048
  6.0 0.0 copy-start.6
  6.0 0.7 %copy-done.6 = f32[256]{0:T(256)S(1)} copy-done((f32[256]{0:T(256)S(1)}, f32[256]{0:T(256)}, u32[]{:S(2)}) %copy-start.6) | copy-done | bytes 1048
  6.7 31.1 %shard_map.73 = (bf16[4,8,256,256]{3,2,1,0:T(8,128)(2,1)S(1)}, bf16[2,256,128]{2,1,0:T(8,128)(2,1)S(1)}) custom-call(bf16[4,75,8,256]{3,2,1,0:T(8,128)(2,1)S(1)} %copy-done, s32[75,8,256]{2,1,0:T(8,128)S(1)} %copy-done.2, s32[256]{0:T(256)S(1)} %copy-done.4, bf16[9,75,256]{2,1,0:T(8,128)(2,1)S(1)} %bitcast.3, f32[1,256]{1,0:T(1,128)S(1)} %bitcast.4, ...), custom_call_target="tpu_custom_call" | custom-call | tf_op jit(solution)/shard_map/pallas_call | solution.py:498
  37.8 3.9 %shard_map.74 = bf16[4,256,8,256]{3,2,1,0:T(8,128)(2,1)} custom-call(bf16[4,8,256,256]{3,2,1,0:T(8,128)(2,1)S(1)} %get-tuple-element.7.y_hbm, bf16[2,256,128]{2,1,0:T(8,128)(2,1)S(1)} %get-tuple-element.8.edge_ref), custom_call_target="tpu_custom_call" | custom-call | tf_op jit(solution)/shard_map/pallas_call | solution.py:572
Async XLA Ops:
  0.0 1.3 %copy-start = (bf16[4,75,8,256]{3,2,1,0:T(8,128)(2,1)S(1)}, bf16[4,75,8,256]{3,2,1,0:T(8,128)(2,1)}, u32[]{:S(2)}) copy-start(bf16[4,75,8,256]{3,2,1,0:T(8,128)(2,1)} %state_hbm.1) | copy-start | bytes 3686404
  1.3 1.3 %copy-start.1 = (bf16[9,256,256]{2,1,0:T(8,128)(2,1)S(1)}, bf16[9,256,256]{2,1,0:T(8,128)(2,1)}, u32[]{:S(2)}) copy-start(bf16[9,256,256]{2,1,0:T(8,128)(2,1)} %k2_hbm.1) | copy-start | bytes 3538948
  2.6 1.1 %copy-start.2 = (s32[75,8,256]{2,1,0:T(8,128)S(1)}, s32[75,8,256]{2,1,0:T(8,128)}, u32[]{:S(2)}) copy-start(s32[75,8,256]{2,1,0:T(8,128)} %mask_hbm.1) | copy-start | bytes 1843204
  3.6 1.0 %copy-start.3 = (bf16[9,256,75]{1,2,0:T(8,128)(2,1)S(1)}, bf16[9,256,75]{1,2,0:T(8,128)(2,1)}, u32[]{:S(2)}) copy-start(bf16[9,256,75]{1,2,0:T(8,128)(2,1)} %param.10) | copy-start | bytes 1036804
  4.6 0.7 %copy-start.4 = (s32[256]{0:T(256)S(1)}, s32[256]{0:T(256)}, u32[]{:S(2)}) copy-start(s32[256]{0:T(256)} %fold_ref.1) | copy-start | bytes 3076
  5.3 0.7 %copy-start.5 = (f32[256]{0:T(256)S(1)}, f32[256]{0:T(256)}, u32[]{:S(2)}) copy-start(f32[256]{0:T(256)} %param.11) | copy-start | bytes 3076
  6.0 0.7 %copy-start.6 = (f32[256]{0:T(256)S(1)}, f32[256]{0:T(256)}, u32[]{:S(2)}) copy-start(f32[256]{0:T(256)} %param.13) | copy-start | bytes 3076

commit v7 on v5

--- a/solution.py
+++ b/solution.py
@@ -40,18 +40,17 @@
     return pairs
 
 
-def prepare(state_ref, mask_ref, x_ref, t_ref):
-    for s in range(SAMPLES):
-        for h in range(2):
-            cut = slice(h * 128, (h + 1) * 128)
-            t_ref[s, h, CIN * ROWS : (CIN + 1) * ROWS, :] = mask_ref[0, :, cut].astype(F32)
-            t_ref[s, h, (CIN + 1) * ROWS : (CIN + 4) * ROWS, :] = jnp.ones((3 * ROWS, 128), F32)
-            t_ref[s, h, (CIN + 4) * ROWS :, :] = jnp.zeros(((CPAD - CIN - 4) * ROWS, 128), F32)
-            masked = state_ref[s, :, :, cut].astype(F32) * mask_ref[:, :, cut].astype(F32)
-            t_ref[s, h, : CIN * ROWS, :] = masked.reshape(CIN * ROWS, 128)
-            for r in range(ROWS):
-                at = s * COLS + h * 128
-                x_ref[r + 2, :, at : at + 128] = t_ref[s, h, pl.ds(r, CPAD, stride=ROWS), :].astype(BF16)
+def prepare(state_ref, mask_ref, x_ref, t_ref, s):
+    for h in range(2):
+        cut = slice(h * 128, (h + 1) * 128)
+        t_ref[s, h, CIN * ROWS : (CIN + 1) * ROWS, :] = mask_ref[0, :, cut].astype(F32)
+        t_ref[s, h, (CIN + 1) * ROWS : (CIN + 4) * ROWS, :] = jnp.ones((3 * ROWS, 128), F32)
+        t_ref[s, h, (CIN + 4) * ROWS :, :] = jnp.zeros(((CPAD - CIN - 4) * ROWS, 128), F32)
+        masked = state_ref[s, :, :, cut].astype(F32) * mask_ref[:, :, cut].astype(F32)
+        t_ref[s, h, : CIN * ROWS, :] = masked.reshape(CIN * ROWS, 128)
+        for r in range(ROWS):
+            at = s * COLS + h * 128
+            x_ref[r + 2, :, at : at + 128] = t_ref[s, h, pl.ds(r, CPAD, stride=ROWS), :].astype(BF16)
 
 
 def piece(i):
@@ -196,10 +195,13 @@
 ):
     loads = [
         pltpu.make_async_copy(src, dst, load_sem.at[n])
-        for n, (src, dst) in enumerate(((mask_hbm, mask_ref), (state_hbm, state_ref), (k1_hbm, k1_raw), (k2_hbm, k2_ref)))
+        for n, (src, dst) in enumerate(
+            [(mask_hbm, mask_ref), (k1_hbm, k1_raw), (k2_hbm, k2_ref)]
+            + [(state_hbm.at[s], state_ref.at[s]) for s in range(SAMPLES)]
+        )
     ]
-    for load in loads:
-        load.start()
+    for n in (1, 0, 3, 4, 5, 6, 2):
+        loads[n].start()
     lon = lax.axis_index("lon")
     lat = lax.axis_index("lat")
     right, left = lax.rem(lon + 1, NLON), lax.rem(lon + NLON - 1, NLON)
@@ -234,9 +236,13 @@
     pl.when(is_relay)(lambda: [greet(NLAT // 2 - 1, lon), greet(NLAT // 2, lon)] and None)
     pl.when(jnp.logical_or(is_low, is_high))(lambda: greet(0, lon))
 
+    loads[1].wait()
+    stack_taps(k1_raw, b1_ref, k1_pad, k1_ref, False)
+    bias2 = wide_bias(b2_ref)
     loads[0].wait()
-    loads[1].wait()
-    prepare(state_ref, mask_ref, x_ref, t_ref)
+    for s in range(SAMPLES):
+        loads[3 + s].wait()
+        prepare(state_ref, mask_ref, x_ref, t_ref, s)
 
     def hidden(r, which=0):
         hidden_row(x_ref, xb_ref, hb_ref, k1_ref, which, r)
@@ -337,23 +343,20 @@
 
     pl.when(has[1])(lambda: up.start())
     pl.when(direct)(lambda: down.start())
+    for r in range(2, 2 + ROWS):
+        shift_row(x_ref, xb_ref, r)
+
     pairs = edge_pairs(x_ref, range(2, 2 + ROWS), [jnp.zeros((CPAD, 128), F32)] * 4)
     for n, pair in enumerate((pairs[0], pairs[3])):
         sp_ref[n] = jnp.transpose(jnp.concatenate([pair, jnp.zeros((48, 128), F32)], 0)).astype(BF16)
+    for r in range(2, HROWS - 2):
+        hidden(r)
     for d in (-1, 0, 1):
         def go(d=d):
             edge[d][0].start()
             edge[d][1].start()
         when(has[d], go)
     loads[2].wait()
-    stack_taps(k1_raw, b1_ref, k1_pad, k1_ref, False)
-    bias2 = wide_bias(b2_ref)
-    for r in range(2, 2 + ROWS):
-        shift_row(x_ref, xb_ref, r)
-
-    for r in range(2, HROWS - 2):
-        hidden(r)
-    loads[3].wait()
     output(2)
 
     @pl.when(top)
@@ -405,6 +408,12 @@
     output(1)
     output(0)
 
+    for d in (-1, 0, 1):
+        def got(d=d):
+            edge[-d][0].wait_recv()
+            edge[-d][1].wait_recv()
+        when(has[d], got)
+
     pl.when(jnp.logical_and(has[1], jnp.logical_not(is_low)))(lambda: down.wait_recv())
 
     @pl.when(is_low)
@@ -431,12 +440,6 @@
     hidden(ROWS + 1, jnp.where(top, 1, 0))
     output(6)
     output(7)
-
-    for d in (-1, 0, 1):
-        def got(d=d):
-            edge[-d][0].wait_recv()
-            edge[-d][1].wait_recv()
-        when(has[d], got)
     pairs = edge_pairs(x_ref, (0, 1, 10, 11), pairs)
     lane = lanes_of((CPAD, 128))
 
@@ -525,7 +528,7 @@
             pltpu.VMEM((NLON, 16, 128), BF16),
             pltpu.VMEM((NLON, 16, 128), BF16),
             pltpu.VMEM((2, CPAD, 128), F32),
-            dma((4,)), dma((ROWS,)),
+            dma((3 + SAMPLES,)), dma((ROWS,)),
             dma((2,)), dma((2,)), dma((SAMPLES,)), dma((SAMPLES,)), dma((SAMPLES,)), dma((SAMPLES,)), dma((6,)), dma((6,)),
             dma((NLON,)), dma((NLON,)), dma((NLON,)), dma((NLON,)), dma((NLON,)), dma((NLON,)),
         ],
@@ -555,13 +558,13 @@
         loads[n].wait()
         if n + AHEAD < len(loads):
             loads[n + AHEAD].start()
+        rows = []
         for r in range(ROWS):
             at = 8 * r + 2 * s
             low = at_first * (pltpu.roll(first, 128 - at, 1) if at else first)
             high = at_last * pltpu.roll(last, 126 - at, 1)
-            y_ref[n, r, :, :128] = y_ref[n, r, :, :128] + low
-            y_ref[n, r, :, 128:] = y_ref[n, r, :, 128:] + high
-        out_ref[n] = jnp.swapaxes(y_ref[n], 0, 1)
+            rows.append(jnp.concatenate([y_ref[n, r, :, :128] + low, y_ref[n, r, :, 128:] + high], 1))
+        out_ref[n] = jnp.swapaxes(jnp.stack(rows), 0, 1)
         stores[n].start()
     for store in stores:
         store.wait()

time: 36.9 us -> 35.9 us (0.973)
  Pallas kernels: 36.3 us -> 35.3 us
    pallas_call x1, Pallas kernels: 30.8 us -> 30 us  [main(): pl.pallas_call(main_kernel, out_shape=(jax.ShapeDtypeStruct((SAMPLES, ROW...]
where the time goes in v7:
time: 35.9 us; the launch traced here: 35.5 us
  Pallas kernels  35.3 us (98%)
    pallas_call x1, Pallas kernels, main(): pl.pallas_call(main_kernel, out_shape=(jax.ShapeDtypeStruct((SAMPLES, ROW...  30 us
    pallas_call x1, Pallas kernels, order(): pl.pallas_call(order_kernel, out_shape=jax.ShapeDtypeStruct((SAMPLES, HID...  5.36 us

profile of v7, /device:TPU:14, one launch (start us, length us, event | category | flops | bytes accessed | tf_op | source)
XLA Modules:
  0.0 35.5 jit_solution(10481904118845973696)
XLA Ops:
  0.0 30.0 %shard_map.73 = (bf16[4,8,256,256]{3,2,1,0:T(8,128)(2,1)}, bf16[2,256,128]{2,1,0:T(8,128)(2,1)}) custom-call(bf16[4,75,8,256]{3,2,1,0:T(8,128)(2,1)} %state_hbm.1, s32[75,8,256]{2,1,0:T(8,128)} %mask_hbm.1, s32[256]{0:T(256)} %fold_ref.1, bf16[9,75,256]{2,1,0:T(8,128)(2,1)} %bitcast.3, f32[1,256]{1,0:T(1,128)} %bitcast.4, bf16[9,256,256]{2,1,0:T(8,128)(2,1)} %k2_hbm.1, ...), custom_call_target="tpu_custom_call" | custom-call | tf_op jit(solution)/shard_map/pallas_call | solution.py:500
  30.0 5.4 %shard_map.74 = bf16[4,256,8,256]{3,2,1,0:T(8,128)(2,1)} custom-call(bf16[4,8,256,256]{3,2,1,0:T(8,128)(2,1)} %get-tuple-element.7.y_hbm, bf16[2,256,128]{2,1,0:T(8,128)(2,1)} %get-tuple-element.8.edge_ref), custom_call_target="tpu_custom_call" | custom-call | tf_op jit(solution)/shard_map/pallas_call | solution.py:574
